TPU v7x, 256 devices: a whole 4x4x8 slice. The times are simulated.
256 devices in a mesh: elem: 64 (over z, y, core), lev: 4 (over x).
Axes of the slice: x: 4, y: 4, z: 8, core: 2. Of those that a mesh axis runs over, the one named last changes fastest.
Arguments:
- winds: float32 [2, 8, 16, 16384], P(None, 'lev', None, 'elem'), may hold values from -6 to 6
- surface: float32 [16, 16384], P(None, 'elem'), may hold values from -6 to 6
- thickness: float32 [8], P('lev'), may hold values from 0.05 to 0.5
- tracers: float32 [8, 9, 16384, 224], P('lev', None, 'elem'), may hold values from 0.1 to 10
- neighbours: int32 [4, 16384], P(None, 'elem'), may hold values from 0 to 16383, as said below
- rotations: int32 [4, 16384], P(None, 'elem'), may hold values from 4 to 7, as said below
- live_count: int32 [64], P('elem'), may hold values from 128 to 256, as said below
Outputs:
- winds_out: float32 [2, 8, 16, 16384], P(None, 'lev', None, 'elem')
- surface_out: float32 [16, 16384], P(None, 'elem')
- tracers_out: float32 [8, 9, 16384, 224], P('lev', None, 'elem')
Inputs may be any that keep to these rules, and one draw needn't show every extreme that they name: `live_count`: the live slots of a device are its first ones and their number is a multiple of 16; one device has all 256 live, one has exactly half of them, each has at least half. `neighbours`: neighbours of live slots are live slots and mutual: if g is across edge k of e with code r, then e is across edge r mod 4 of g. A neighbour on another device is one of the last 16 live slots of the device before, or one of the first 16 slots of the device after, along the curve, which closes into a loop. `rotations`: codes of live slots agree with the neighbours from both sides.
All inputs are finite; a program needn't handle non-finite values.
Results may differ from a plain program's by a relative error of at most 0.0003.
Values sent between devices are 32-bit elements; how exact they have to be, the bound alone decides.
No kernel may reach another device: no remote copies, remote signals or barrier semaphores. Data moves between devices by JAX's collectives and lax.ppermute only.
A program may use at most 128 MiB of HBM per device.

v0:
```python
import jax
import jax.numpy as jnp
import numpy as np
from jax import lax
from jax.sharding import PartitionSpec as P

PRECISE = lax.Precision.HIGHEST
STEP = 0.1
COURANT = 0.45
NODE_EDGES = [[0, 1, 2, 3], [3, 7, 11, 15], [15, 14, 13, 12], [12, 8, 4, 0]]
CELL_EDGES = [[0, 1, 2], [2, 5, 8], [8, 7, 6], [6, 3, 0]]
BORDER_NODES = [0, 1, 2, 3, 4, 7, 8, 11, 12, 13, 14, 15]
BORDER_CELLS = [0, 1, 2, 3, 5, 6, 7, 8]


def with_halo(shard, sides, width):
    for axis, dim in sides:
        devices, length = (lax.axis_size(axis), shard.shape[dim])
        up = [(i, (i + 1) % devices) for i in range(devices)]
        down = [(j, i) for i, j in up]
        last = lax.slice_in_dim(shard, length - width, length, axis=dim)
        leading = lax.slice_in_dim(shard, 0, width, axis=dim)
        before = lax.ppermute(last, axis, up)
        after = lax.ppermute(leading, axis, down)
        shard = jnp.concatenate([before, shard, after], axis=dim)
    return shard


def node_tables():
    points = np.array([-1.0, -(0.2**0.5), 0.2**0.5, 1.0])
    products = np.array(
        [np.prod([points[a] - points[k] for k in range(4) if k != a]) for a in range(4)]
    )
    derivative = np.zeros((4, 4))
    for source in range(4):
        for target in range(4):
            if source != target:
                derivative[source, target] = (
                    products[source] / products[target] / (points[source] - points[target])
                )
        derivative[source, source] = sum(
            (1.0 / (points[source] - points[k]) for k in range(4) if k != source)
        )
    identity = np.eye(4)
    along_x = np.kron(identity, derivative)
    along_y = np.kron(derivative, identity)
    centers = np.array([-2.0 / 3.0, 0.0, 2.0 / 3.0])
    lagrange = np.array(
        [
            [
                np.prod([(t - points[k]) / (points[b] - points[k]) for k in range(4) if k != b])
                for b in range(4)
            ]
            for t in centers
        ]
    )
    to_cells = np.kron(lagrange, lagrange)
    scatter = np.zeros((16, 16))
    for facing in range(4):
        for station in range(4):
            scatter[NODE_EDGES[facing][station], 4 * facing + station] = 1.0
    multiplicity = 1.0 + scatter.sum(axis=1)
    return [
        jnp.asarray(np.float32(table))
        for table in (along_x, along_y, to_cells, scatter, multiplicity)
    ]


def ghost_index(slots, codes, edge_lists, border_list, count):
    span = len(edge_lists[0])
    result = []
    for facing in range(4):
        for station in range(span):
            source = jnp.zeros_like(codes[facing])
            for code_value in range(8):
                remote = code_value % 4
                mirrored = station if code_value < 4 else span - 1 - station
                source = source + jnp.where(
                    codes[facing] == code_value, border_list.index(edge_lists[remote][mirrored]), 0
                )
            result.append(source * count + slots[facing])
    return jnp.stack(result)


def divergence(winds, along_x, along_y):
    return jnp.einsum("nm,lme->lne", along_x, winds[0], precision=PRECISE) + jnp.einsum(
        "nm,lme->lne", along_y, winds[1], precision=PRECISE
    )


def remap_cells(values, ghosts, shift_x, shift_y):
    result = []
    for cell_row in range(3):
        for cell_col in range(3):
            cell_index = 3 * cell_row + cell_col
            middle = values[..., cell_index, :, :]
            west_side = (
                values[..., cell_index - 1, :, :]
                if cell_col > 0
                else ghosts[..., 9 + 2 - cell_row, :, :]
            )
            east_side = (
                values[..., cell_index + 1, :, :]
                if cell_col < 2
                else ghosts[..., 3 + cell_row, :, :]
            )
            south_side = (
                values[..., cell_index - 3, :, :] if cell_row > 0 else ghosts[..., cell_col, :, :]
            )
            north_side = (
                values[..., cell_index + 3, :, :]
                if cell_row < 2
                else ghosts[..., 6 + 2 - cell_col, :, :]
            )
            slope_x = 0.5 * (east_side - west_side)
            curve_x = 0.5 * (east_side + west_side) - middle
            slope_y = 0.5 * (north_side - south_side)
            curve_y = 0.5 * (north_side + south_side) - middle
            moved_x = shift_x[..., cell_index, :, :]
            moved_y = shift_y[..., cell_index, :, :]
            result.append(
                middle
                - slope_x * moved_x
                + curve_x * moved_x * moved_x
                - slope_y * moved_y
                + curve_y * moved_y * moved_y
            )
    return jnp.stack(result, axis=-3)


def body(winds, surface, thickness, tracers, neighbours, rotations, live_count):
    count = winds.shape[3]
    levels = winds.shape[1]
    tracer_total = tracers.shape[3]
    elem_total = lax.axis_size("elem")
    position_here = lax.axis_index("elem")
    live_here = live_count[0]
    along_x, along_y, to_cells, scatter, multiplicity = node_tables()
    owners = neighbours // count
    local_slot = neighbours % count
    relative = (owners - position_here + 1) % elem_total
    slots = relative * count + local_slot
    stride = 3 * count
    tracer_border = jnp.concatenate([tracers[:, 0:4], tracers[:, 5:9]], axis=1)
    tracer_halo = with_halo(tracer_border, (("elem", 2),), count)
    partial_column = jnp.einsum(
        "l,lne->ne", thickness, divergence(winds, along_x, along_y), precision=PRECISE
    )
    column = lax.psum(partial_column, "lev")
    surface_star = surface - STEP * column
    grad_x = jnp.dot(along_x, surface_star, precision=PRECISE)
    grad_y = jnp.dot(along_y, surface_star, precision=PRECISE)
    winds_star = winds - STEP * jnp.stack([grad_x, grad_y])[:, None]
    picked = winds_star[:, :, jnp.array(BORDER_NODES), :].reshape(2 * levels, 12, count)
    border = jnp.concatenate([picked, surface_star[None, jnp.array(BORDER_NODES), :]], axis=0)
    rows_total = border.shape[0]
    node_halo = with_halo(border, (("elem", 2),), count)
    node_index = ghost_index(slots, rotations, NODE_EDGES, BORDER_NODES, stride)
    ghosts = jnp.take(node_halo.reshape(rows_total, 12 * stride), node_index, axis=1)
    values = jnp.concatenate(
        [winds_star.reshape(2 * levels, 16, count), surface_star[None]], axis=0
    )
    summed = (
        values + jnp.einsum("ng,rge->rne", scatter, ghosts, precision=PRECISE)
    ) / multiplicity[None, :, None]
    winds_new = summed[: 2 * levels].reshape(2, levels, 16, count)
    surface_new = summed[2 * levels]
    shift_x = COURANT * jnp.tanh(
        jnp.einsum("cn,lne->lce", to_cells, winds_new[0], precision=PRECISE)
    )
    shift_y = COURANT * jnp.tanh(
        jnp.einsum("cn,lne->lce", to_cells, winds_new[1], precision=PRECISE)
    )
    cell_index = ghost_index(slots, rotations, CELL_EDGES, BORDER_CELLS, stride).reshape(-1)
    cell_ghosts = jnp.take(
        tracer_halo.reshape(levels, 8 * stride, tracer_total), cell_index, axis=1
    )
    cell_ghosts = cell_ghosts.reshape(levels, 12, count, tracer_total)
    moved = remap_cells(tracers, cell_ghosts, shift_x[..., None], shift_y[..., None])
    live = jnp.arange(count, dtype=jnp.int32) < live_here
    winds_out = jnp.where(live, winds_new, 0.0)
    surface_out = jnp.where(live, surface_new, 0.0)
    tracers_out = jnp.where(live[:, None], moved, 0.0)
    return (winds_out, surface_out, tracers_out)


def solution(mesh):
    in_specs = (
        P(None, "lev", None, "elem"),
        P(None, "elem"),
        P("lev"),
        P("lev", None, "elem", None),
        P(None, "elem"),
        P(None, "elem"),
        P("elem"),
    )
    out_specs = (P(None, "lev", None, "elem"), P(None, "elem"), P("lev", None, "elem", None))
    return jax.shard_map(body, mesh=mesh, in_specs=in_specs, out_specs=out_specs, check_vma=False)
```

profile of v0, /device:TPU:4, one launch (start us, length us, event | category | flops | bytes accessed | tf_op | source)
XLA Modules:
  0.0 163.2 jit_solution(13515854877816419537)
XLA Ops:
  0.6 2.4 %fusion.27 = (f32[2,4,256,224]{2,3,1,0:T(8,128)S(1)}, f32[2,4,256,224]{2,3,1,0:T(8,128)S(1)}) fusion(f32[2,9,256,224]{2,3,1,0:T(8,128)} %param.17), kind=kLoop, calls=%fused_computation.194 | loop fusion | bytes 7340032 | tf_op jit(solution)/shard_map/slice | solution.py:144
  3.2 1.2 copy-done.2
  4.4 2.2 %pad_maximum_fusion.1 = f32[2,8,256,224]{2,3,1,0:T(8,128)} fusion(f32[2,4,256,224]{2,3,1,0:T(8,128)S(1)} %get-tuple-element.51, f32[2,4,256,224]{2,3,1,0:T(8,128)S(1)} %get-tuple-element.50), kind=kLoop, calls=%fused_computation.5 | loop fusion | flops 917504 | bytes 7340032 | tf_op jit(solution)/shard_map/concatenate | solution.py:144
  6.6 7.7 %collective-permute-start.3 = (f32[2,8,256,224]{2,3,1,0:T(8,128)}, f32[2,8,256,224]{2,3,1,0:T(8,128)}, u32[]{:S(2)}, u32[]{:S(2)}) collective-permute-start(f32[2,8,256,224]{2,3,1,0:T(8,128)} %pad_maximum_fusion.1), channel_id=1, source_target_pairs={{4,0},{8,4},{12,8},{16,12},{20,16},{24,20},{28,24},{32,28},{36,32}... | collective-permute-start | bytes 11010056 | tf_op jit(solution)/shard_map/ppermute | solution.py:24
  15.0 14.7 %psum.7 = f32[16,256]{1,0:T(8,128)S(1)} all-reduce(f32[16,256]{1,0:T(8,128)S(1)} %bitcast.193), channel_id=1, replica_groups=mesh['elem'=64,'lev'=4] {'lev'}, use_global_device_ids=true, to_apply=%region_0.1 | all-reduce | flops 4096 | bytes 32768 | tf_op jit(solution)/shard_map/psum | solution.py:149
  30.7 0.6 gather_fusion
  31.4 0.7 pad_maximum_fusion.3
  32.1 5.1 %collective-permute-start.1 = (f32[5,12,256]{2,0,1:T(8,128)}, f32[5,12,256]{2,0,1:T(8,128)}, u32[]{:S(2)}, u32[]{:S(2)}) collective-permute-start(f32[5,12,256]{2,0,1:T(8,128)} %pad_maximum_fusion.3), channel_id=1, source_target_pairs={{4,0},{8,4},{12,8},{16,12},{20,16},{24,20},{28,24},{32,28},{36,32}... | collective-permute-start | bytes 184328 | tf_op jit(solution)/shard_map/ppermute | solution.py:24
  37.3 3.8 %fusion.26 = (f32[2,1,256,224]{2,3,1,0:T(8,128)}, f32[2,1,256,224]{2,3,1,0:T(8,128)}, f32[2,1,256,224]{2,3,1,0:T(8,128)S(1)}, f32[2,1,256,224]{2,3,1,0:T(8,128)}...) fusion(f32[2,9,256,224]{2,3,1,0:T(8,128)} %param.17), kind=kLoop, calls=%fused_computation.193 | loop fusion | bytes 8257536 | tf_op jit(solution)/shard_map/slice | solution.py:111
  43.4 2.0 %copy.91 = f32[2,1,256,224]{3,2,1,0:T(8,128)} copy(f32[2,1,256,224]{2,3,1,0:T(8,128)} %get-tuple-element.48) | data formatting | bytes 917504
  45.5 2.0 %copy.93 = f32[2,1,256,224]{3,2,1,0:T(8,128)} copy(f32[2,1,256,224]{2,3,1,0:T(8,128)} %get-tuple-element.47) | data formatting | bytes 917504
  47.5 1.0 copy.90
  48.5 1.2 copy.96
  49.7 1.0 copy.94
  50.7 1.2 copy.98
  51.9 1.0 copy.100
  52.9 1.2 copy.102
  54.1 2.0 %copy.104 = f32[2,1,256,224]{3,2,1,0:T(8,128)} copy(f32[2,1,256,224]{2,3,1,0:T(8,128)} %get-tuple-element.41) | data formatting | bytes 917504
  57.4 1.7 %pad_maximum_fusion.2 = f32[5,12,768]{2,0,1:T(8,128)} fusion(f32[5,12,256]{2,0,1:T(8,128)} %collective-permute-done.1, f32[1,12,256]{2,0,1:T(1,128)S(1)} %copy.59, f32[4,12,256]{2,0,1:T(4,128)S(1)} %reshape.756, f32[5,12,256]{2,0,1:T(8,128)} %collective-permute-done), kind=kLoop, calls=%fused_computation.29 | loop fusion | flops 138240 | bytes 368640 | tf_op jit(solution)/shard_map/concatenate | solution.py:25
  59.1 3.9 %copy.60 = f32[5,12,768]{0,2,1:T(8,128)} copy(f32[5,12,768]{2,0,1:T(8,128)} %pad_maximum_fusion.2) | data formatting | bytes 368640 | tf_op jit(solution)/shard_map/concatenate | solution.py:25
  63.0 16.5 %gather_fusion.2 = f32[4096,5]{1,0:T(8,128)} fusion(f32[5,9216]{0,1:T(8,128)} %bitcast.183, s32[4096]{0:T(1024)S(1)} %copy-done.11), kind=kCustom, calls=%fused_computation.2 | custom fusion | bytes 180224 | tf_op jit(solution)/shard_map/jit(_take)/gather | solution.py:159
  79.5 2.9 %copy.61 = f32[16,256,5]{1,0,2:T(8,128)} copy(f32[16,256,5]{2,1,0:T(8,128)} %bitcast.185) | data formatting | bytes 163840 | tf_op jit(solution)/shard_map/jit(_take)/gather | solution.py:159
  82.4 1.1 fusion.1
  84.6 1.2 fusion.17
  85.9 1.3 broadcast_select_fusion.2
  87.1 8.3 %pad_maximum_fusion = f32[2,8,768,224]{2,3,1,0:T(8,128)} fusion(f32[2,8,256,224]{2,3,1,0:T(8,128)} %collective-permute-done.3, f32[2,4,256,224]{2,3,1,0:T(8,128)} %copy-done.2, f32[2,4,256,224]{2,3,1,0:T(8,128)S(1)} %get-tuple-element.50, f32[2,8,256,224]{2,3,1,0:T(8,128)} %collective-permute-done.2), kind=kLoop, calls=%fused_computation.4 | loop fusion | flops 8257536 | bytes 22020096 | tf_op jit(solution)/shard_map/concatenate | solution.py:25
  95.5 19.0 %copy.87 = f32[2,8,768,224]{3,0,2,1:T(2,128)} copy(f32[2,8,768,224]{2,3,1,0:T(8,128)} %pad_maximum_fusion) | data formatting | bytes 22020096 | tf_op jit(solution)/shard_map/reshape | solution.py:176
  114.4 30.3 %gather_fusion.3 = f32[3072,2,224]{2,1,0:T(2,128)} fusion(f32[2,6144,224]{2,0,1:T(2,128)} %bitcast.180, s32[3072]{0:T(1024)S(1)} %copy-done.12), kind=kCustom, calls=%fused_computation.3 | custom fusion | bytes 11022336 | tf_op jit(solution)/shard_map/jit(_take)/gather | solution.py:175
  144.7 3.3 %copy.66 = f32[2,3072,224]{2,1,0:T(8,128)S(1)} copy(f32[2,3072,224]{2,0,1:T(2,128)} %bitcast.181) | data formatting | bytes 11010048 | tf_op jit(solution)/shard_map/jit(_take)/gather | solution.py:175
  148.1 0.8 broadcast_select_fusion
  154.6 2.8 %broadcast_select_fusion.1 = f32[2,9,256,224]{3,2,1,0:T(8,128)} fusion(f32[2,9,256,224]{3,2,1,0:T(8,128)S(1)} %add_dynamic-update-slice_fusion, pred[256]{0:T(512)(128)(4,1)S(1)} %copy-done.22), kind=kLoop, calls=%fused_computation.7 | loop fusion | flops 1032192 | bytes 8257792 | tf_op jit(solution)/shard_map/jit(_where)/select_n | solution.py:183
  157.4 5.8 %copy.84 = f32[2,9,256,224]{2,3,1,0:T(8,128)} copy(f32[2,9,256,224]{3,2,1,0:T(8,128)} %broadcast_select_fusion.1) | data formatting | bytes 8257536
  (125 shorter events, 11.3 us)
Async XLA Ops:
  0.6 14.1 %copy-start = (f32[2]{0:T(128)S(1)}, f32[2]{0:T(128)}, u32[]{:S(2)}) copy-start(f32[2]{0:T(128)} %param.16) | copy-start | bytes 28
  3.0 1.3 copy-start.2
  3.0 11.3 %copy-start.9 = (f32[2,2,16,256]{3,2,1,0:T(8,128)S(1)}, f32[2,2,16,256]{3,2,1,0:T(8,128)}, u32[]{:S(2)}) copy-start(f32[2,2,16,256]{3,2,1,0:T(8,128)} %param.14) | copy-start | bytes 196612
  3.1 11.3 %copy-start.20 = (f32[16,16,1]{1,0,2:T(8,128)S(1)}, f32[16,16,1]{1,0,2:T(8,128)}, u32[]{:S(2)}) copy-start(f32[16,16,1]{1,0,2:T(8,128)} %constant.148) | copy-start | bytes 3076
  3.1 11.5 %copy-start.21 = (f32[16,16,1]{1,0,2:T(8,128)S(1)}, f32[16,16,1]{1,0,2:T(8,128)}, u32[]{:S(2)}) copy-start(f32[16,16,1]{1,0,2:T(8,128)} %constant.149) | copy-start | bytes 3076
  3.1 26.6 %copy-start.15 = (f32[16,256]{1,0:T(8,128)S(1)}, f32[16,256]{1,0:T(8,128)}, u32[]{:S(2)}) copy-start(f32[16,256]{1,0:T(8,128)} %param.15) | copy-start | bytes 49156
  3.1 26.6 %copy-start.19 = (f32[16,16]{1,0:T(8,128)S(1)}, f32[16,16]{1,0:T(8,128)}, u32[]{:S(2)}) copy-start(f32[16,16]{1,0:T(8,128)} %constant.132.clone) | copy-start | bytes 3076
  3.1 26.8 %copy-start.18 = (f32[16,16]{1,0:T(8,128)S(1)}, f32[16,16]{1,0:T(8,128)}, u32[]{:S(2)}) copy-start(f32[16,16]{1,0:T(8,128)} %constant.131.clone) | copy-start | bytes 3076
  3.1 27.0 %copy-start.25 = (s32[12]{0:T(128)S(1)}, s32[12]{0:T(128)}, u32[]{:S(2)}) copy-start(s32[12]{0:T(128)} %constant.146) | copy-start | bytes 148
  3.1 34.0 %copy-start.23 = (s32[4,256]{1,0:T(4,128)S(1)}, s32[4,256]{1,0:T(4,128)}, u32[]{:S(2)}) copy-start(s32[4,256]{1,0:T(4,128)} %param.18) | copy-start | bytes 12292
  3.1 34.0 %copy-start.10 = (s32[4,256]{1,0:T(4,128)S(1)}, s32[4,256]{1,0:T(4,128)}, u32[]{:S(2)}) copy-start(s32[4,256]{1,0:T(4,128)} %param.19) | copy-start | bytes 12292
  6.6 80.5 %collective-permute-start.2 = (f32[2,8,256,224]{2,3,1,0:T(8,128)}, f32[2,8,256,224]{2,3,1,0:T(8,128)}, u32[]{:S(2)}, u32[]{:S(2)}) collective-permute-start(f32[2,8,256,224]{2,3,1,0:T(8,128)} %pad_maximum_fusion.1), channel_id=1, source_target_pairs={{0,4},{4,8},{8,12},{12,16},{16,20},{20,24},{24,28},{28,32},{32,36}... | collective-permute-start | bytes 11010056 | tf_op jit(solution)/shard_map/ppermute | solution.py:23
  6.6 80.5 %collective-permute-start.3 = (f32[2,8,256,224]{2,3,1,0:T(8,128)}, f32[2,8,256,224]{2,3,1,0:T(8,128)}, u32[]{:S(2)}, u32[]{:S(2)}) collective-permute-start(f32[2,8,256,224]{2,3,1,0:T(8,128)} %pad_maximum_fusion.1), channel_id=1, source_target_pairs={{4,0},{8,4},{12,8},{16,12},{20,16},{24,20},{28,24},{32,28},{36,32}... | collective-permute-start | bytes 11010056 | tf_op jit(solution)/shard_map/ppermute | solution.py:24
  32.1 25.3 %collective-permute-start = (f32[5,12,256]{2,0,1:T(8,128)}, f32[5,12,256]{2,0,1:T(8,128)}, u32[]{:S(2)}, u32[]{:S(2)}) collective-permute-start(f32[5,12,256]{2,0,1:T(8,128)} %pad_maximum_fusion.3), channel_id=1, source_target_pairs={{0,4},{4,8},{8,12},{12,16},{16,20},{20,24},{24,28},{28,32},{32,36}... | collective-permute-start | bytes 184328 | tf_op jit(solution)/shard_map/ppermute | solution.py:23
  32.1 25.3 %collective-permute-start.1 = (f32[5,12,256]{2,0,1:T(8,128)}, f32[5,12,256]{2,0,1:T(8,128)}, u32[]{:S(2)}, u32[]{:S(2)}) collective-permute-start(f32[5,12,256]{2,0,1:T(8,128)} %pad_maximum_fusion.3), channel_id=1, source_target_pairs={{4,0},{8,4},{12,8},{16,12},{20,16},{24,20},{28,24},{32,28},{36,32}... | collective-permute-start | bytes 184328 | tf_op jit(solution)/shard_map/ppermute | solution.py:24
  59.1 3.9 %copy-start.11 = (s32[4096]{0:T(1024)S(1)}, s32[4096]{0:T(1024)}, u32[]{:S(2)}) copy-start(s32[4096]{0:T(1024)} %broadcast_clamp_fusion) | copy-start | bytes 49156
  59.1 23.3 %copy-start.17 = (f32[16,16,1]{1,0,2:T(8,128)S(1)}, f32[16,16,1]{1,0,2:T(8,128)}, u32[]{:S(2)}) copy-start(f32[16,16,1]{1,0,2:T(8,128)} %constant.150) | copy-start | bytes 3076
  59.1 23.3 %copy-start.24 = (f32[16]{0:T(128)S(1)}, f32[16]{0:T(128)}, u32[]{:S(2)}) copy-start(f32[16]{0:T(128)} %constant.141) | copy-start | bytes 196
  59.1 24.4 %copy-start.13 = (f32[9,16,1]{1,0,2:T(8,128)S(1)}, f32[9,16,1]{1,0,2:T(8,128)}, u32[]{:S(2)}) copy-start(f32[9,16,1]{1,0,2:T(8,128)} %constant.151) | copy-start | bytes 1732
  95.5 19.0 %copy-start.12 = (s32[3072]{0:T(1024)S(1)}, s32[3072]{0:T(1024)}, u32[]{:S(2)}) copy-start(s32[3072]{0:T(1024)} %broadcast_clamp_fusion.1) | copy-start | bytes 36868
  144.7 3.3 %copy-start.14 = (pred[12,256]{1,0:T(8,128)(4,1)S(1)}, pred[12,256]{1,0:T(8,128)(4,1)}, u32[]{:S(2)}) copy-start(pred[12,256]{1,0:T(8,128)(4,1)} %compare_and_fusion) | copy-start | bytes 9220
  148.0 1.0 copy-start.3
  148.0 1.2 copy-start.4
  148.1 1.3 copy-start.8
  148.1 1.3 copy-start.16
  148.1 1.8 %copy-start.7 = (f32[2,1,256,224]{3,2,1,0:T(8,128)S(1)}, f32[2,1,256,224]{3,2,1,0:T(8,128)}, u32[]{:S(2)}) copy-start(f32[2,1,256,224]{3,2,1,0:T(8,128)} %copy.94) | copy-start | bytes 1376260
  149.4 1.7 %copy-start.6 = (f32[2,1,256,224]{3,2,1,0:T(8,128)S(1)}, f32[2,1,256,224]{3,2,1,0:T(8,128)}, u32[]{:S(2)}) copy-start(f32[2,1,256,224]{3,2,1,0:T(8,128)} %copy.100) | copy-start | bytes 1376260
  150.5 1.8 %copy-start.5 = (f32[2,1,256,224]{3,2,1,0:T(8,128)S(1)}, f32[2,1,256,224]{3,2,1,0:T(8,128)}, u32[]{:S(2)}) copy-start(f32[2,1,256,224]{3,2,1,0:T(8,128)} %copy.104) | copy-start | bytes 1376260
  152.8 1.8 %copy-start.22 = (pred[256]{0:T(512)(128)(4,1)S(1)}, pred[256]{0:T(512)(128)(4,1)}, u32[]{:S(2)}) copy-start(pred[256]{0:T(512)(128)(4,1)} %iota_compare_fusion) | copy-start | bytes 772
  154.6 8.6 %copy-start.1 = (f32[2]{0:T(128)S(1)}, f32[2]{0:T(128)}, u32[]{:S(2)}) copy-start(f32[2]{0:T(128)} %param.16) | copy-start | bytes 28
where the time goes:
time: 165 us; the launch traced here: 163 us
  local copies, waits for them, and re-layouts  104 us (63%)
  other arithmetic  27 us (16%)
  blocking collectives  14.7 us (9%)
  starting transfers between devices  12.8 us (8%)
  matrix products  2.23 us (1%)
  between operations  1.95 us (1%)
    gather x2, local copies, waits for them, and re-layouts, body(): jnp.take(tracer_halo.reshape(levels, 8 * stride, tracer_total), cell_inde...  33.6 us
    unnamed x65, local copies, waits for them, and re-layouts  20.5 us
    gather x2, local copies, waits for them, and re-layouts, body(): jnp.take(node_halo.reshape(rows_total, 12 * stride), node_index, axis=1)  19.4 us
    reshape x1, local copies, waits for them, and re-layouts, body(): tracer_halo.reshape(levels, 8 * stride, tracer_total)  19 us
    psum x1, blocking collectives, body(): column = lax.psum(partial_column, 'lev')  14.7 us
    ppermute x2, starting transfers between devices, with_halo(): after = lax.ppermute(leading, axis, down)  12.8 us
    concatenate x2, other arithmetic, with_halo(): shard = jnp.concatenate([before, shard, after], axis=dim)  10 us
    unnamed x23, other arithmetic  4.83 us
  transfers between devices with their start and end apart: 4, of which 0 were waited for; matrix products, arithmetic and copies ran while one was open for 32% of the time, Pallas kernels for 0%

commit v1 on v0

v1 whole, which is shorter than its diff:
```python
import functools
import jax
import jax.numpy as jnp
import numpy as np
from jax import lax
from jax.experimental import pallas as pl
from jax.experimental.pallas import tpu as pltpu
from jax.sharding import PartitionSpec as P

STEP = 0.1
COURANT = 0.45
HALO = 16
NODE_EDGES = [[0, 1, 2, 3], [3, 7, 11, 15], [15, 14, 13, 12], [12, 8, 4, 0]]
NODE_RING = [0, 1, 2, 3, 7, 11, 15, 14, 13, 12, 8, 4]
CELL_RING = [0, 1, 2, 5, 8, 7, 6, 3]
FIELDS = 8


def tables():
    points = np.array([-1.0, -(0.2**0.5), 0.2**0.5, 1.0])
    products = np.array(
        [np.prod([points[a] - points[k] for k in range(4) if k != a]) for a in range(4)]
    )
    derivative = np.zeros((4, 4))
    for source in range(4):
        for target in range(4):
            if source != target:
                derivative[source, target] = (
                    products[source] / products[target] / (points[source] - points[target])
                )
        derivative[source, source] = sum(
            (1.0 / (points[source] - points[k]) for k in range(4) if k != source)
        )
    identity = np.eye(4)
    along_x = np.kron(identity, derivative)
    along_y = np.kron(derivative, identity)
    centers = np.array([-2.0 / 3.0, 0.0, 2.0 / 3.0])
    lagrange = np.array(
        [
            [
                np.prod([(t - points[k]) / (points[b] - points[k]) for k in range(4) if k != b])
                for b in range(4)
            ]
            for t in centers
        ]
    )
    return along_x.astype(np.float32), along_y.astype(np.float32), lagrange


def multiplicity(node):
    return 1 + sum(node in edge for edge in NODE_EDGES)


def exact_dot(a, b):
    return jnp.dot(a, b, precision=lax.Precision.HIGHEST, preferred_element_type=jnp.float32)


def column_kernel(thickness_in, matrix_in, winds_in, part, thickness, matrix, winds, sems):
    copies = [
        pltpu.make_async_copy(source, target, sems.at[number])
        for number, (source, target) in enumerate(
            ((winds_in, winds), (matrix_in, matrix), (thickness_in, thickness))
        )
    ]
    for copy in copies:
        copy.start()
    for copy in copies:
        copy.wait()
    levels = winds.shape[1]
    sums = []
    for component in range(2):
        total = thickness[0] * winds[component, 0]
        for level in range(1, levels):
            total = total + thickness[level] * winds[component, level]
        sums.append(total)
    part[...] = exact_dot(matrix[...], jnp.concatenate(sums, axis=0))


def strips(live):
    even = lax.rem(lax.axis_index("elem"), 2) == 0
    start = live[0] - HALO
    tile = start // 128
    lane = start % 128
    return (
        (jnp.where(even, tile, 0), jnp.where(even, lane, 0)),
        (jnp.where(even, 0, tile), jnp.where(even, 0, lane)),
    )


def strip_kernel(live, tracers, order, held, inside, outside, sems):
    del order
    levels, _, tracer_total, _ = tracers.shape
    loads = [
        pltpu.make_async_copy(tracers.at[level], held.at[level], sems.at[level])
        for level in range(levels)
    ]
    for load in loads:
        load.start()
    lane_block = lax.broadcasted_iota(jnp.int32, (8, 128), 1) // HALO
    ends = strips(live)
    for level in range(levels):
        loads[level].wait()
        for target, (tile, lane) in zip((inside, outside), ends):
            lanes = pl.ds(pl.multiple_of(128 * tile, 128), 128)
            shifts = [lax.rem(HALO * place + 128 - lane, 128) for place in range(8)]

            def pack(group, carry, target=target, lanes=lanes, shifts=shifts, level=level):
                base = pl.multiple_of(8 * group, 8)
                packed = None
                for place in range(8):
                    values = held[level, CELL_RING[place], pl.ds(base, 8), lanes]
                    moved = pltpu.roll(values, shifts[place], 1)
                    packed = (
                        moved if packed is None else jnp.where(lane_block == place, moved, packed)
                    )
                target[pl.ds(level * tracer_total + base, 8), :] = packed
                return carry

            lax.fori_loop(0, tracer_total // 8, pack, 0, unroll=4)


def star_kernel(live, matrix, *refs):
    *parts, surface, winds, inside_in, outside_in, star, inside, outside = refs
    del inside_in, outside_in
    levels = winds.shape[1]
    column = parts[0][...]
    for part in parts[1:]:
        column = column + part[...]
    surface_star = surface[...] - STEP * column
    gradient = exact_dot(matrix[...], surface_star)
    for tile in range(2):
        lanes = slice(128 * tile, 128 * tile + 128)
        for component in range(2):
            slope = gradient[16 * component : 16 * component + 16, lanes]
            for level in range(levels):
                star[tile, pl.ds(levels * component + level, 16, stride=FIELDS), :] = (
                    winds[component, level, :, lanes] - STEP * slope
                )
        for field in range(2 * levels, FIELDS):
            star[tile, pl.ds(field, 16, stride=FIELDS), :] = surface_star[:, lanes]
    lane_block = lax.broadcasted_iota(jnp.int32, (FIELDS, 128), 1) // HALO
    base = inside.shape[0] - 2 * FIELDS
    for target, (tile, at) in zip((inside, outside), strips(live)):
        for block in range(2):
            packed = None
            for place in range(min(8, 12 - 8 * block)):
                node = NODE_RING[8 * block + place]
                values = star[tile, pl.ds(FIELDS * node, FIELDS), :]
                moved = pltpu.roll(values, lax.rem(HALO * place + 128 - at, 128), 1)
                packed = moved if packed is None else jnp.where(lane_block == place, moved, packed)
            target[pl.ds(base + FIELDS * block, FIELDS), :] = packed


def add_edges(nodes, codes, ring):
    for edge in range(4):
        code = codes[edge]
        found = ring(edge)
        for place in range(4):
            value = found((3 - place) % 12)
            for other in range(1, 4):
                value = jnp.where(code == other, found((3 * other + 3 - place) % 12), value)
            node = NODE_EDGES[edge][place]
            nodes[node] = nodes[node] + value


def rows_of(ref, edge, tile):
    return jnp.broadcast_to(ref[pl.ds(edge, 1), pl.ds(128 * tile, 128)], (FIELDS, 128))


def lane_gather(values, index):
    return jnp.take_along_axis(values, index, axis=1, mode="promise_in_bounds")


def weights(nodes, live, tile, factors):
    lagrange = tables()[2]
    rows = [
        [
            sum(float(lagrange[x, n]) * nodes[4 * y + n] for n in range(4))
            for x in range(3)
        ]
        for y in range(4)
    ]
    lanes = pl.ds(128 * tile, 128)
    lane = lax.broadcasted_iota(jnp.int32, (FIELDS, 128), 1) + 128 * tile
    row = lax.broadcasted_iota(jnp.int32, (FIELDS, 128), 0)
    alive = lane < live
    for y in range(3):
        for x in range(3):
            value = sum(float(lagrange[y, n]) * rows[n][x] for n in range(4))
            shift = COURANT * jnp.tanh(value)
            square = shift * shift
            low = 0.5 * (square + shift)
            high = 0.5 * (square - shift)
            middle = 1.0 - square - pltpu.roll(square, 6, 0)
            sides = jnp.where(row < 4, low, pltpu.roll(high, 4, 0))
            at = 16 * (3 * y + x)
            factors[pl.ds(at, 8), lanes] = jnp.where(alive, sides, 0.0)
            factors[pl.ds(at + 8, 8), lanes] = jnp.where(alive, middle, 0.0)


def picks(line, wanted):
    return jnp.where(line == wanted, 1.0, 0.0).astype(jnp.bfloat16)


def split(values):
    high = values.astype(jnp.bfloat16)
    low = (values - high.astype(jnp.float32)).astype(jnp.bfloat16)
    return jnp.concatenate([high, low], axis=1)


def inner_kernel(neighbours, rotations, star, held, order, sums, ghosts, remote):
    del order
    levels, _, tracer_total, count = held.shape
    me = lax.axis_index("elem")
    for tile in range(2):
        nodes = [star[tile, pl.ds(FIELDS * n, FIELDS), :] for n in range(16)]
        codes = [rows_of(rotations, edge, tile) & 3 for edge in range(4)]

        def ring(edge, tile=tile):
            slots = rows_of(neighbours, edge, tile)
            own = slots // count == me
            local = slots % count
            within = local % 128
            upper = local >= 128
            kept = {}

            def found(place):
                if place not in kept:
                    at = pl.ds(FIELDS * NODE_RING[place], FIELDS)
                    both = jnp.where(
                        upper, lane_gather(star[1, at, :], within), lane_gather(star[0, at, :], within)
                    )
                    kept[place] = jnp.where(own, both, 0.0)
                return kept[place]

            return found

        add_edges(nodes, codes, ring)
        for n in range(16):
            sums[tile, pl.ds(FIELDS * n, FIELDS), :] = nodes[n]

    devices = lax.axis_size("elem")
    line = lax.broadcasted_iota(jnp.int32, (count, count), 0)
    slots = neighbours[...]
    own = slots // count == me
    after = slots // count == lax.rem(me + 1, devices)
    codes = rotations[...] & 3
    near = jnp.where(own, slots % count, -1)
    pickers = []
    for edge in range(4):
        picker = picks(line, near[edge : edge + 1])
        pickers.append(jnp.concatenate([picker, picker], axis=0))
    for place in range(3):
        source = HALO * ((2 * codes + 2 - place) & 7) + slots % HALO + jnp.where(after, 128, 0)
        source = jnp.where(own, -1, source)
        for edge in range(4):
            remote[3 * edge + place] = picks(line, source[edge : edge + 1])
    chosen = [
        [jnp.broadcast_to(codes[edge : edge + 1] == other, (8, count)) for other in range(4)]
        for edge in range(4)
    ]
    for level in range(levels):
        for start in range(0, tracer_total, BLOCK):
            rows = pl.ds(start, BLOCK)
            border = jnp.concatenate([split(held[level, cell, rows, :]) for cell in CELL_RING], axis=0)
            for edge in range(4):
                ring = jnp.dot(border, pickers[edge], preferred_element_type=jnp.float32)
                for at in range(0, BLOCK, 8):
                    for place in range(3):
                        value = None
                        for other in range(4):
                            base = BLOCK * ((2 * other + 2 - place) % 8) + at
                            found = ring[base : base + 8]
                            value = found if value is None else jnp.where(chosen[edge][other], found, value)
                        ghosts[level, 3 * edge + place, pl.ds(start + at, 8), :] = value


def outer_kernel(
    live,
    neighbours,
    rotations,
    sums,
    held,
    near,
    remote,
    inside,
    outside,
    winds_out,
    surface_out,
    moved,
    means,
    factors,
    ghosts,
    done,
    sems,
):
    levels, _, tracer_total, count = held.shape
    me = lax.axis_index("elem")
    devices = lax.axis_size("elem")
    even = lax.rem(me, 2) == 0
    base = levels * tracer_total

    def both_sides(rows):
        left, right = inside[rows, :], outside[rows, :]
        return jnp.where(even, right, left), jnp.where(even, left, right)

    strip = split(jnp.concatenate(both_sides(pl.ds(0, base)), axis=1))
    for number in range(12):
        picker = remote[number]
        found = jnp.dot(
            strip, jnp.concatenate([picker, picker], axis=0), preferred_element_type=jnp.float32
        )
        for level in range(levels):
            ghosts[level, number] = near[level, number] + found[level * tracer_total : (level + 1) * tracer_total]

    node_halo = [both_sides(pl.ds(base + FIELDS * block, FIELDS)) for block in range(2)]
    for tile in range(2):
        nodes = [sums[tile, pl.ds(FIELDS * n, FIELDS), :] for n in range(16)]
        for edge in range(4):
            slots = rows_of(neighbours, edge, tile)
            code = rows_of(rotations, edge, tile) & 3
            owner = slots // count
            other = owner != me
            after = owner == lax.rem(me + 1, devices)
            for place in range(4):
                spot = 3 * code + 3 - place
                spot = jnp.where(spot >= 12, spot - 12, spot)
                index = HALO * (spot & 7) + (slots & (HALO - 1))
                high = spot >= 8
                value = jnp.where(
                    high, lane_gather(node_halo[1][1], index), lane_gather(node_halo[0][1], index)
                )
                if tile == 0:
                    behind = jnp.where(
                        high, lane_gather(node_halo[1][0], index), lane_gather(node_halo[0][0], index)
                    )
                    value = jnp.where(after, value, behind)
                node = NODE_EDGES[edge][place]
                nodes[node] = nodes[node] + jnp.where(other, value, 0.0)
        nodes = [nodes[n] * (1.0 / multiplicity(n)) for n in range(16)]
        weights(nodes, live[0], tile, factors)
        lane = lax.broadcasted_iota(jnp.int32, (FIELDS, 128), 1) + 128 * tile
        for n in range(16):
            means[tile, pl.ds(FIELDS * n, FIELDS), :] = jnp.where(lane < live[0], nodes[n], 0.0)
        lanes = pl.ds(128 * tile, 128)
        for component in range(2):
            for level in range(levels):
                winds_out[component, level, :, lanes] = means[
                    tile, pl.ds(levels * component + level, 16, stride=FIELDS), :
                ]
        surface_out[:, lanes] = means[tile, pl.ds(2 * levels, 16, stride=FIELDS), :]

    chunk = CHUNK
    for level in range(levels):

        def groups(group, carry, level=level):
            rows = [pl.ds(pl.multiple_of(chunk * group + 8 * i, 8), 8) for i in range(chunk // 8)]
            for tile in range(2):
                lanes = pl.ds(128 * tile, 128)

                def ghost(edge, place):
                    return [ghosts[level, 3 * edge + place, r, lanes] for r in rows]

                cells = [[held[level, cell, r, lanes] for r in rows] for cell in range(9)]
                for row in range(3):
                    for col in range(3):
                        cell = 3 * row + col
                        west = cells[cell - 1] if col > 0 else ghost(3, 2 - row)
                        east = cells[cell + 1] if col < 2 else ghost(1, row)
                        south = cells[cell - 3] if row > 0 else ghost(0, col)
                        north = cells[cell + 3] if row < 2 else ghost(2, 2 - col)
                        factor = [
                            jnp.broadcast_to(factors[pl.ds(16 * cell + at + level, 1), lanes], (8, 128))
                            for at in (0, 2, 4, 6, 8)
                        ]
                        for i, r in enumerate(rows):
                            done[level, cell, r, lanes] = (
                                cells[cell][i] * factor[4]
                                + (west[i] * factor[0] + east[i] * factor[2])
                                + (south[i] * factor[1] + north[i] * factor[3])
                            )
            where = (level, slice(None), pl.ds(pl.multiple_of(chunk * group, 8), chunk))
            pltpu.make_async_copy(done.at[where], moved.at[where], sems.at[level, group]).start()
            return carry

        lax.fori_loop(0, tracer_total // chunk, groups, 0)
    for level in range(levels):
        for group in range(tracer_total // chunk):
            where = (level, slice(None), pl.ds(chunk * group, chunk))
            pltpu.make_async_copy(done.at[where], moved.at[where], sems.at[level, group]).wait()


VMEM = pl.BlockSpec(memory_space=pltpu.VMEM)
SMEM = pl.BlockSpec(memory_space=pltpu.SMEM)
HBM = pl.BlockSpec(memory_space=pltpu.HBM)
ANY = pl.BlockSpec(memory_space=pl.ANY)
LIMIT = pltpu.CompilerParams(vmem_limit_bytes=20 * 1024 * 1024)
CHUNK = 32
BLOCK = 112


def in_hbm(array):
    return pltpu.with_memory_space_constraint(array, pltpu.HBM)


def body(winds, surface, thickness, tracers, neighbours, rotations, live_count):
    levels, _, count, tracer_total = tracers.shape
    along_x, along_y, _ = tables()
    across = jnp.asarray(np.concatenate([along_x, along_y], axis=1))
    down = jnp.asarray(np.concatenate([along_x, along_y], axis=0))
    f32 = functools.partial(jax.ShapeDtypeStruct, dtype=jnp.float32)
    turned = jnp.transpose(tracers, (0, 1, 3, 2))
    pack_shape = (levels * tracer_total + 2 * FIELDS, 128)

    part = pl.pallas_call(
        column_kernel,
        name="column",
        in_specs=[HBM, HBM, HBM],
        out_specs=VMEM,
        out_shape=f32((16, count)),
        scratch_shapes=[
            pltpu.SMEM(thickness.shape, jnp.float32),
            pltpu.VMEM(across.shape, jnp.float32),
            pltpu.VMEM(winds.shape, jnp.float32),
            pltpu.SemaphoreType.DMA((3,)),
        ],
        compiler_params=LIMIT,
    )(in_hbm(thickness), in_hbm(across), in_hbm(winds))

    ranks = lax.axis_size("lev")
    parts = [part]
    for step in range(1, ranks):
        parts.append(lax.ppermute(part, "lev", [(i, i ^ step) for i in range(ranks)]))

    held, inside, outside = pl.pallas_call(
        strip_kernel,
        name="strips",
        in_specs=[SMEM, HBM, ANY],
        out_specs=[VMEM] * 3,
        out_shape=[
            pltpu.VMEM(turned.shape, jnp.float32),
            pltpu.VMEM(pack_shape, jnp.float32),
            pltpu.VMEM(pack_shape, jnp.float32),
        ],
        scratch_shapes=[pltpu.SemaphoreType.DMA((levels,))],
        compiler_params=LIMIT,
    )(live_count, in_hbm(turned), part)

    star, inside, outside = pl.pallas_call(
        star_kernel,
        name="star",
        in_specs=[SMEM, VMEM] + [VMEM] * (ranks + 4),
        out_specs=[VMEM] * 3,
        out_shape=[
            pltpu.VMEM((2, 16 * FIELDS, 128), jnp.float32),
            pltpu.VMEM(pack_shape, jnp.float32),
            pltpu.VMEM(pack_shape, jnp.float32),
        ],
        input_output_aliases={ranks + 4: 1, ranks + 5: 2},
        compiler_params=LIMIT,
    )(live_count, down, *parts, surface, winds, inside, outside)

    devices = lax.axis_size("elem")
    outside_in = lax.ppermute(
        outside, "elem", [(i, (((i + 1) % devices ^ 1) - 1) % devices) for i in range(devices)]
    )
    inside_in = lax.ppermute(inside, "elem", [(i, i ^ 1) for i in range(devices)])

    sums, ghosts, remote = pl.pallas_call(
        inner_kernel,
        name="inner",
        in_specs=[VMEM, VMEM, VMEM, VMEM, ANY],
        out_specs=[VMEM, VMEM, VMEM],
        out_shape=[
            pltpu.VMEM((2, 16 * FIELDS, 128), jnp.float32),
            pltpu.VMEM((levels, 12, tracer_total, count), jnp.float32),
            pltpu.VMEM((12, count, count), jnp.bfloat16),
        ],
        compiler_params=LIMIT,
    )(neighbours, rotations, star, held, star)

    winds_out, surface_out, moved = pl.pallas_call(
        outer_kernel,
        name="outer",
        in_specs=[SMEM] + [VMEM] * 8,
        out_specs=[VMEM, VMEM, HBM],
        out_shape=[f32(winds.shape), f32(surface.shape), f32(turned.shape)],
        scratch_shapes=[
            pltpu.VMEM((2, 16 * FIELDS, 128), jnp.float32),
            pltpu.VMEM((9 * 16, count), jnp.float32),
            pltpu.VMEM((levels, 12, tracer_total, count), jnp.float32),
            pltpu.VMEM(turned.shape, jnp.float32),
            pltpu.SemaphoreType.DMA((levels, tracer_total // CHUNK)),
        ],
        compiler_params=LIMIT,
    )(live_count, neighbours, rotations, sums, held, ghosts, remote, inside_in, outside_in)
    return winds_out, surface_out, jnp.transpose(moved, (0, 1, 3, 2))


def solution(mesh):
    in_specs = (
        P(None, "lev", None, "elem"),
        P(None, "elem"),
        P("lev"),
        P("lev", None, "elem", None),
        P(None, "elem"),
        P(None, "elem"),
        P("elem"),
    )
    out_specs = (P(None, "lev", None, "elem"), P(None, "elem"), P("lev", None, "elem", None))
    return jax.shard_map(body, mesh=mesh, in_specs=in_specs, out_specs=out_specs, check_vma=False)
```

time: 165 us -> 30 us (0.18)
  local copies, waits for them, and re-layouts: 104 us -> 0.02 us
  other arithmetic: 27 us -> 0 us
  Pallas kernels: 0 us -> 15.7 us
  blocking collectives: 14.7 us -> 0 us
  matrix products: 2.23 us -> 0 us
    gather x6 -> x0, local copies, waits for them, and re-layouts: 54.2 us -> none  [the longest x2 33.6 us: body(): jnp.take(tracer_halo.reshape(levels, 8 * stride, tracer_total), cell_inde...]
    unnamed x65 -> x10, local copies, waits for them, and re-layouts: 20.5 us -> 0.02 us
    reshape x2 -> x0, local copies, waits for them, and re-layouts: 19 us -> none  [the longest x1 19 us: body(): tracer_halo.reshape(levels, 8 * stride, tracer_total)]
    pallas_call x0 -> x5, Pallas kernels: none -> 15.7 us  [the longest x1 5.2 us: body(): pl.pallas_call(outer_kernel, name='outer', in_specs=[SMEM] + [VMEM] * 8,...]
    psum x1 -> x0, blocking collectives: 14.7 us -> none  [body(): column = lax.psum(partial_column, 'lev')]
    concatenate x4 -> x0, other arithmetic: 13 us -> none  [the longest x2 10 us: with_halo(): shard = jnp.concatenate([before, shard, after], axis=dim)]
    slice x4 -> x0, local copies, waits for them, and re-layouts: 6.18 us -> none  [the longest x1 3.77 us: remap_cells(): values[..., cell_index + 3, :, :]]
    select_n x6 -> x0, other arithmetic: 6.08 us -> none  [the longest x1 2.77 us: body(): tracers_out = jnp.where(live[:, None], moved, 0.0)]
  transfers between devices with their start and end apart: 4 -> 5, of which waited for: 0 -> 0; matrix products, arithmetic and copies ran while one was open for 32% -> 0% of each run, Pallas kernels for 0% -> 31%
where the time goes in v1:
time: 30 us; the launch traced here: 29.9 us
  Pallas kernels  15.7 us (52%)
  starting transfers between devices  12.7 us (42%)
  between operations  1.43 us (5%)
    ppermute x1, starting transfers between devices, body(): lax.ppermute(outside, 'elem', [(i, (((i + 1) % devices ^ 1) - 1) % device...  8.41 us
    pallas_call x1, Pallas kernels, body(): pl.pallas_call(outer_kernel, name='outer', in_specs=[SMEM] + [VMEM] * 8,...  5.2 us
    pallas_call x1, Pallas kernels, body(): pl.pallas_call(inner_kernel, name='inner', in_specs=[VMEM, VMEM, VMEM, VM...  4.73 us
    pallas_call x1, Pallas kernels, body(): pl.pallas_call(strip_kernel, name='strips', in_specs=[SMEM, HBM, ANY], ou...  4.45 us
    ppermute x3, starting transfers between devices, body(): lax.ppermute(part, 'lev', [(i, i ^ step) for i in range(ranks)])  4.18 us
    pallas_call x1, Pallas kernels, body(): pl.pallas_call(column_kernel, name='column', in_specs=[HBM, HBM, HBM], ou...  1.07 us
  transfers between devices with their start and end apart: 5, of which 0 were waited for; matrix products, arithmetic and copies ran while one was open for 0% of the time, Pallas kernels for 31%

profile of v1, /device:TPU:4, one launch (start us, length us, event | category | flops | bytes accessed | tf_op | source)
XLA Modules:
  0.0 29.9 jit_solution(2360987497713567967)
XLA Ops:
  0.6 0.0 copy-start.2
  0.6 0.0 copy-start
  0.7 0.0 copy-start.1
  0.7 0.0 copy-start.4
  0.7 0.0 copy-start.3
  0.7 1.1 %column.1.order.refs_0_ = f32[16,256]{1,0:T(8,128)S(1)} custom-call(f32[2]{0:T(128)} %thickness_in.1, f32[16,32]{1,0:T(8,128)} %constant.4.clone.matrix_in, f32[2,2,16,256]{3,2,1,0:T(8,128)} %refs_5_.1), custom_call_target="tpu_custom_call" | custom-call | tf_op jit(solution)/shard_map/column/pallas_call | solution.py:415
  1.8 0.6 %collective-permute-start.2 = (f32[16,256]{1,0:T(8,128)S(1)}, f32[16,256]{1,0:T(8,128)S(1)}, u32[]{:S(2)}, u32[]{:S(2)}) collective-permute-start(f32[16,256]{1,0:T(8,128)S(1)} %column.1.order.refs_0_), channel_id=1, source_target_pairs={{0,3},{1,2},{2,1},{3,0},{4,7},{5,6},{6,5},{7,4},{8,11},{9,10},{10,... | collective-permute-start | bytes 49160 | tf_op jit(solution)/shard_map/ppermute | solution.py:433
  2.4 2.7 %collective-permute-start.1 = (f32[16,256]{1,0:T(8,128)S(1)}, f32[16,256]{1,0:T(8,128)S(1)}, u32[]{:S(2)}, u32[]{:S(2)}) collective-permute-start(f32[16,256]{1,0:T(8,128)S(1)} %column.1.order.refs_0_), channel_id=1, source_target_pairs={{0,2},{1,3},{2,0},{3,1},{4,6},{5,7},{6,4},{7,5},{8,10},{9,11},{10,... | collective-permute-start | bytes 49160 | tf_op jit(solution)/shard_map/ppermute | solution.py:433
  5.1 0.8 %collective-permute-start = (f32[16,256]{1,0:T(8,128)S(1)}, f32[16,256]{1,0:T(8,128)S(1)}, u32[]{:S(2)}, u32[]{:S(2)}) collective-permute-start(f32[16,256]{1,0:T(8,128)S(1)} %column.1.order.refs_0_), channel_id=1, source_target_pairs={{0,1},{1,0},{2,3},{3,2},{4,5},{5,4},{6,7},{7,6},{8,9},{9,8},{10,11... | collective-permute-start | bytes 49160 | tf_op jit(solution)/shard_map/ppermute | solution.py:433
  6.6 4.5 %strips.1 = (f32[2,9,224,256]{3,2,1,0:T(8,128)S(1)}, f32[464,128]{1,0:T(8,128)S(1)}, f32[464,128]{1,0:T(8,128)S(1)}) custom-call(s32[1]{0:T(128)S(6)} %copy.16.live, f32[2,9,224,256]{3,2,1,0:T(8,128)} %bitcast.2, f32[16,256]{1,0:T(8,128)S(1)} %column.1.order.refs_0_), custom_call_target="tpu_custom_call" | custom-call | tf_op jit(solution)/shard_map/strips/pallas_call | solution.py:435
  11.1 0.0 collective-permute-done.2.refs_3_
  11.1 0.0 collective-permute-done.1.refs_2_
  11.1 0.0 collective-permute-done.refs_1_
  11.1 0.0 copy-done.2
  11.1 0.0 copy-done
  11.1 0.0 copy-done.1
  11.1 0.3 star.1
  11.4 0.1 collective-permute-start.3
  11.5 8.4 %collective-permute-start.4 = (f32[464,128]{1,0:T(8,128)S(1)}, f32[464,128]{1,0:T(8,128)S(1)}, u32[]{:S(2)}, u32[]{:S(2)}) collective-permute-start(f32[464,128]{1,0:T(8,128)S(1)} %get-tuple-element.23), channel_id=1, source_target_pairs={{0,252},{4,8},{8,4},{12,16},{16,12},{20,24},{24,20},{28,32},{32,28... | collective-permute-start | bytes 712712 | tf_op jit(solution)/shard_map/ppermute | solution.py:464
  19.9 0.0 copy-done.4
  19.9 0.0 copy-done.3
  19.9 4.7 %inner.1 = (f32[2,128,128]{2,1,0:T(8,128)S(1)}, f32[2,12,224,256]{3,2,1,0:T(8,128)S(1)}, bf16[12,256,256]{2,1,0:T(8,128)(2,1)S(1)}) custom-call(s32[4,256]{1,0:T(4,128)S(1)} %copy-done.3, s32[4,256]{1,0:T(4,128)S(1)} %copy-done.4, f32[2,128,128]{2,1,0:T(8,128)S(1)} %get-tuple-element.17.star.order, f32[2,9,224,256]{3,2,1,0:T(8,128)S(1)} %get-tuple-element.18.held, ...), custom_call_target="tpu_custom_call" | custom-call | tf_op jit(solution)/shard_map/inner/pallas_call | solution.py:469
  24.6 0.0 collective-permute-done.3.inside
  24.6 0.0 collective-permute-done.4.outside
  24.7 5.2 %outer.1 = (f32[2,2,16,256]{3,2,1,0:T(8,128)}, f32[16,256]{1,0:T(8,128)}, f32[2,9,224,256]{3,2,1,0:T(8,128)}) custom-call(s32[1]{0:T(128)S(6)} %copy.16.live, s32[4,256]{1,0:T(4,128)S(1)} %copy-done.3, s32[4,256]{1,0:T(4,128)S(1)} %copy-done.4, f32[2,128,128]{2,1,0:T(8,128)S(1)} %get-tuple-element.19.sums, f32[2,9,224,256]{3,2,1,0:T(8,128)S(1)} %get-tuple-element.18.held, ...), custom_call_target="tpu_custom_call" | custom-call | tf_op jit(solution)/shard_map/outer/pallas_call | solution.py:482
Async XLA Ops:
  0.6 10.5 %copy-start.2 = (f32[32,16]{1,0:T(8,128)S(1)}, f32[32,16]{1,0:T(8,128)}, u32[]{:S(2)}) copy-start(f32[32,16]{1,0:T(8,128)} %constant.5.clone.matrix) | copy-start | bytes 6148
  0.6 10.5 %copy-start = (f32[2,2,16,256]{3,2,1,0:T(8,128)S(1)}, f32[2,2,16,256]{3,2,1,0:T(8,128)}, u32[]{:S(2)}) copy-start(f32[2,2,16,256]{3,2,1,0:T(8,128)} %refs_5_.1) | copy-start | bytes 196612
  0.7 10.5 %copy-start.1 = (f32[16,256]{1,0:T(8,128)S(1)}, f32[16,256]{1,0:T(8,128)}, u32[]{:S(2)}) copy-start(f32[16,256]{1,0:T(8,128)} %refs_4_.1) | copy-start | bytes 49156
  0.7 19.2 %copy-start.4 = (s32[4,256]{1,0:T(4,128)S(1)}, s32[4,256]{1,0:T(4,128)}, u32[]{:S(2)}) copy-start(s32[4,256]{1,0:T(4,128)} %rotations.3) | copy-start | bytes 12292
  0.7 19.2 %copy-start.3 = (s32[4,256]{1,0:T(4,128)S(1)}, s32[4,256]{1,0:T(4,128)}, u32[]{:S(2)}) copy-start(s32[4,256]{1,0:T(4,128)} %neighbours.3) | copy-start | bytes 12292
  1.8 9.3 %collective-permute-start.2 = (f32[16,256]{1,0:T(8,128)S(1)}, f32[16,256]{1,0:T(8,128)S(1)}, u32[]{:S(2)}, u32[]{:S(2)}) collective-permute-start(f32[16,256]{1,0:T(8,128)S(1)} %column.1.order.refs_0_), channel_id=1, source_target_pairs={{0,3},{1,2},{2,1},{3,0},{4,7},{5,6},{6,5},{7,4},{8,11},{9,10},{10,... | collective-permute-start | bytes 49160 | tf_op jit(solution)/shard_map/ppermute | solution.py:433
  2.4 8.7 %collective-permute-start.1 = (f32[16,256]{1,0:T(8,128)S(1)}, f32[16,256]{1,0:T(8,128)S(1)}, u32[]{:S(2)}, u32[]{:S(2)}) collective-permute-start(f32[16,256]{1,0:T(8,128)S(1)} %column.1.order.refs_0_), channel_id=1, source_target_pairs={{0,2},{1,3},{2,0},{3,1},{4,6},{5,7},{6,4},{7,5},{8,10},{9,11},{10,... | collective-permute-start | bytes 49160 | tf_op jit(solution)/shard_map/ppermute | solution.py:433
  5.1 6.0 %collective-permute-start = (f32[16,256]{1,0:T(8,128)S(1)}, f32[16,256]{1,0:T(8,128)S(1)}, u32[]{:S(2)}, u32[]{:S(2)}) collective-permute-start(f32[16,256]{1,0:T(8,128)S(1)} %column.1.order.refs_0_), channel_id=1, source_target_pairs={{0,1},{1,0},{2,3},{3,2},{4,5},{5,4},{6,7},{7,6},{8,9},{9,8},{10,11... | collective-permute-start | bytes 49160 | tf_op jit(solution)/shard_map/ppermute | solution.py:433
  11.4 13.3 %collective-permute-start.3 = (f32[464,128]{1,0:T(8,128)S(1)}, f32[464,128]{1,0:T(8,128)S(1)}, u32[]{:S(2)}, u32[]{:S(2)}) collective-permute-start(f32[464,128]{1,0:T(8,128)S(1)} %get-tuple-element.22), channel_id=1, source_target_pairs={{0,4},{4,0},{8,12},{12,8},{16,20},{20,16},{24,28},{28,24},{32,36},... | collective-permute-start | bytes 712712 | tf_op jit(solution)/shard_map/ppermute | solution.py:467
  11.5 13.2 %collective-permute-start.4 = (f32[464,128]{1,0:T(8,128)S(1)}, f32[464,128]{1,0:T(8,128)S(1)}, u32[]{:S(2)}, u32[]{:S(2)}) collective-permute-start(f32[464,128]{1,0:T(8,128)S(1)} %get-tuple-element.23), channel_id=1, source_target_pairs={{0,252},{4,8},{8,4},{12,16},{16,12},{20,24},{24,20},{28,32},{32,28... | collective-permute-start | bytes 712712 | tf_op jit(solution)/shard_map/ppermute | solution.py:464

commit v2 on v1

--- a/solution.py
+++ b/solution.py
@@ -76,9 +76,13 @@
     part[...] = exact_dot(matrix[...], jnp.concatenate(sums, axis=0))
 
 
+def first_of(ref):
+    return ref[...][0]
+
+
 def strips(live):
     even = lax.rem(lax.axis_index("elem"), 2) == 0
-    start = live[0] - HALO
+    start = first_of(live) - HALO
     tile = start // 128
     lane = start % 128
     return (
@@ -87,40 +91,49 @@
     )
 
 
-def strip_kernel(live, tracers, order, held, inside, outside, sems):
+def picks(line, wanted):
+    return jnp.where(line == wanted, 1.0, 0.0).astype(jnp.bfloat16)
+
+
+def split(values):
+    high = values.astype(jnp.bfloat16)
+    low = (values - high.astype(jnp.float32)).astype(jnp.bfloat16)
+    return jnp.concatenate([high, low], axis=1)
+
+
+def strip_kernel(live, tracers, order, held, border, inside, outside, sems):
     del order
-    levels, _, tracer_total, _ = tracers.shape
+    levels, _, tracer_total, count = tracers.shape
     loads = [
         pltpu.make_async_copy(tracers.at[level], held.at[level], sems.at[level])
         for level in range(levels)
     ]
     for load in loads:
         load.start()
-    lane_block = lax.broadcasted_iota(jnp.int32, (8, 128), 1) // HALO
-    ends = strips(live)
+    line = lax.broadcasted_iota(jnp.int32, (count, 256), 0)
+    lane = lax.broadcasted_iota(jnp.int32, (count, 256), 1)
+    starts = [128 * tile + at for tile, at in strips(live)]
+    picker = picks(line, jnp.where(lane < 128, starts[0], starts[1]) + lane % HALO)
+    picker = jnp.concatenate([picker, picker], axis=0)
+    part = (lax.broadcasted_iota(jnp.int32, (BLOCK, 256), 1) % 128) // HALO
     for level in range(levels):
         loads[level].wait()
-        for target, (tile, lane) in zip((inside, outside), ends):
-            lanes = pl.ds(pl.multiple_of(128 * tile, 128), 128)
-            shifts = [lax.rem(HALO * place + 128 - lane, 128) for place in range(8)]
-
-            def pack(group, carry, target=target, lanes=lanes, shifts=shifts, level=level):
-                base = pl.multiple_of(8 * group, 8)
-                packed = None
-                for place in range(8):
-                    values = held[level, CELL_RING[place], pl.ds(base, 8), lanes]
-                    moved = pltpu.roll(values, shifts[place], 1)
-                    packed = (
-                        moved if packed is None else jnp.where(lane_block == place, moved, packed)
-                    )
-                target[pl.ds(level * tracer_total + base, 8), :] = packed
-                return carry
-
-            lax.fori_loop(0, tracer_total // 8, pack, 0, unroll=4)
+        for block in range(tracer_total // BLOCK):
+            rows = pl.ds(BLOCK * block, BLOCK)
+            for place, cell in enumerate(CELL_RING):
+                border[level, block, pl.ds(BLOCK * place, BLOCK), :] = split(held[level, cell, rows, :])
+            found = jnp.dot(border[level, block], picker, preferred_element_type=jnp.float32)
+            packed = found[:BLOCK]
+            for place in range(1, 8):
+                packed = jnp.where(part == place, found[BLOCK * place : BLOCK * (place + 1)], packed)
+            rows = pl.ds(level * tracer_total + BLOCK * block, BLOCK)
+            inside[rows, :] = packed[:, :128]
+            outside[rows, :] = packed[:, 128:]
 
 
 def star_kernel(live, matrix, *refs):
-    *parts, surface, winds, inside_in, outside_in, star, inside, outside = refs
+    *parts, surface, winds, neighbours, rotations, border, inside_in, outside_in = refs[:-4]
+    star, inside, outside, ghosts = refs[-4:]
     del inside_in, outside_in
     levels = winds.shape[1]
     column = parts[0][...]
@@ -150,6 +163,10 @@
                 packed = moved if packed is None else jnp.where(lane_block == place, moved, packed)
             target[pl.ds(base + FIELDS * block, FIELDS), :] = packed
 
+    @pl.when(lax.axis_index("elem") == 0)
+    def _():
+        near_ghosts(neighbours, rotations, border, ghosts, range(1))
+
 
 def add_edges(nodes, codes, ring):
     for edge in range(4):
@@ -198,19 +215,38 @@
             factors[pl.ds(at + 8, 8), lanes] = jnp.where(alive, middle, 0.0)
 
 
-def picks(line, wanted):
-    return jnp.where(line == wanted, 1.0, 0.0).astype(jnp.bfloat16)
-
-
-def split(values):
-    high = values.astype(jnp.bfloat16)
-    low = (values - high.astype(jnp.float32)).astype(jnp.bfloat16)
-    return jnp.concatenate([high, low], axis=1)
-
-
-def inner_kernel(neighbours, rotations, star, held, order, sums, ghosts, remote):
-    del order
-    levels, _, tracer_total, count = held.shape
+def near_ghosts(neighbours, rotations, border, ghosts, which):
+    count = ghosts.shape[3]
+    me = lax.axis_index("elem")
+    line = lax.broadcasted_iota(jnp.int32, (count, count), 0)
+    slots = neighbours[...]
+    codes = rotations[...] & 3
+    near = jnp.where(slots // count == me, slots % count, -1)
+    pickers = []
+    for edge in range(4):
+        picker = picks(line, near[edge : edge + 1])
+        pickers.append(jnp.concatenate([picker, picker], axis=0))
+    chosen = [
+        [jnp.broadcast_to(codes[edge : edge + 1] == other, (8, count)) for other in range(4)]
+        for edge in range(4)
+    ]
+    for level in which:
+        for block in range(border.shape[1]):
+            for edge in range(4):
+                ring = jnp.dot(border[level, block], pickers[edge], preferred_element_type=jnp.float32)
+                for at in range(0, BLOCK, 8):
+                    for place in range(3):
+                        value = None
+                        for other in range(4):
+                            base = BLOCK * ((2 * other + 2 - place) % 8) + at
+                            found = ring[base : base + 8]
+                            value = found if value is None else jnp.where(chosen[edge][other], found, value)
+                        ghosts[level, 3 * edge + place, pl.ds(BLOCK * block + at, 8), :] = value
+
+
+def inner_kernel(neighbours, rotations, star, border, begun, order, sums, ghosts, remote):
+    del begun, order
+    levels, _, tracer_total, count = ghosts.shape
     me = lax.axis_index("elem")
     for tile in range(2):
         nodes = [star[tile, pl.ds(FIELDS * n, FIELDS), :] for n in range(16)]
@@ -245,34 +281,17 @@
     own = slots // count == me
     after = slots // count == lax.rem(me + 1, devices)
     codes = rotations[...] & 3
-    near = jnp.where(own, slots % count, -1)
-    pickers = []
-    for edge in range(4):
-        picker = picks(line, near[edge : edge + 1])
-        pickers.append(jnp.concatenate([picker, picker], axis=0))
     for place in range(3):
         source = HALO * ((2 * codes + 2 - place) & 7) + slots % HALO + jnp.where(after, 128, 0)
         source = jnp.where(own, -1, source)
         for edge in range(4):
             remote[3 * edge + place] = picks(line, source[edge : edge + 1])
-    chosen = [
-        [jnp.broadcast_to(codes[edge : edge + 1] == other, (8, count)) for other in range(4)]
-        for edge in range(4)
-    ]
-    for level in range(levels):
-        for start in range(0, tracer_total, BLOCK):
-            rows = pl.ds(start, BLOCK)
-            border = jnp.concatenate([split(held[level, cell, rows, :]) for cell in CELL_RING], axis=0)
-            for edge in range(4):
-                ring = jnp.dot(border, pickers[edge], preferred_element_type=jnp.float32)
-                for at in range(0, BLOCK, 8):
-                    for place in range(3):
-                        value = None
-                        for other in range(4):
-                            base = BLOCK * ((2 * other + 2 - place) % 8) + at
-                            found = ring[base : base + 8]
-                            value = found if value is None else jnp.where(chosen[edge][other], found, value)
-                        ghosts[level, 3 * edge + place, pl.ds(start + at, 8), :] = value
+
+    @pl.when(me != 0)
+    def _():
+        near_ghosts(neighbours, rotations, border, ghosts, range(1))
+
+    near_ghosts(neighbours, rotations, border, ghosts, range(1, levels))
 
 
 def outer_kernel(
@@ -290,7 +309,8 @@
     moved,
     means,
     factors,
-    ghosts,
+    winds_new,
+    surface_new,
     done,
     sems,
 ):
@@ -298,20 +318,12 @@
     me = lax.axis_index("elem")
     devices = lax.axis_size("elem")
     even = lax.rem(me, 2) == 0
+    alive = first_of(live)
     base = levels * tracer_total
 
     def both_sides(rows):
         left, right = inside[rows, :], outside[rows, :]
         return jnp.where(even, right, left), jnp.where(even, left, right)
-
-    strip = split(jnp.concatenate(both_sides(pl.ds(0, base)), axis=1))
-    for number in range(12):
-        picker = remote[number]
-        found = jnp.dot(
-            strip, jnp.concatenate([picker, picker], axis=0), preferred_element_type=jnp.float32
-        )
-        for level in range(levels):
-            ghosts[level, number] = near[level, number] + found[level * tracer_total : (level + 1) * tracer_total]
 
     node_halo = [both_sides(pl.ds(base + FIELDS * block, FIELDS)) for block in range(2)]
     for tile in range(2):
@@ -338,56 +350,59 @@
                 node = NODE_EDGES[edge][place]
                 nodes[node] = nodes[node] + jnp.where(other, value, 0.0)
         nodes = [nodes[n] * (1.0 / multiplicity(n)) for n in range(16)]
-        weights(nodes, live[0], tile, factors)
+        weights(nodes, alive, tile, factors)
         lane = lax.broadcasted_iota(jnp.int32, (FIELDS, 128), 1) + 128 * tile
         for n in range(16):
-            means[tile, pl.ds(FIELDS * n, FIELDS), :] = jnp.where(lane < live[0], nodes[n], 0.0)
+            means[tile, pl.ds(FIELDS * n, FIELDS), :] = jnp.where(lane < alive, nodes[n], 0.0)
         lanes = pl.ds(128 * tile, 128)
         for component in range(2):
             for level in range(levels):
-                winds_out[component, level, :, lanes] = means[
+                winds_new[component, level, :, lanes] = means[
                     tile, pl.ds(levels * component + level, 16, stride=FIELDS), :
                 ]
-        surface_out[:, lanes] = means[tile, pl.ds(2 * levels, 16, stride=FIELDS), :]
-
-    chunk = CHUNK
-    for level in range(levels):
-
-        def groups(group, carry, level=level):
-            rows = [pl.ds(pl.multiple_of(chunk * group + 8 * i, 8), 8) for i in range(chunk // 8)]
-            for tile in range(2):
-                lanes = pl.ds(128 * tile, 128)
-
-                def ghost(edge, place):
-                    return [ghosts[level, 3 * edge + place, r, lanes] for r in rows]
-
-                cells = [[held[level, cell, r, lanes] for r in rows] for cell in range(9)]
-                for row in range(3):
-                    for col in range(3):
-                        cell = 3 * row + col
-                        west = cells[cell - 1] if col > 0 else ghost(3, 2 - row)
-                        east = cells[cell + 1] if col < 2 else ghost(1, row)
-                        south = cells[cell - 3] if row > 0 else ghost(0, col)
-                        north = cells[cell + 3] if row < 2 else ghost(2, 2 - col)
-                        factor = [
-                            jnp.broadcast_to(factors[pl.ds(16 * cell + at + level, 1), lanes], (8, 128))
-                            for at in (0, 2, 4, 6, 8)
-                        ]
-                        for i, r in enumerate(rows):
-                            done[level, cell, r, lanes] = (
-                                cells[cell][i] * factor[4]
-                                + (west[i] * factor[0] + east[i] * factor[2])
-                                + (south[i] * factor[1] + north[i] * factor[3])
-                            )
-            where = (level, slice(None), pl.ds(pl.multiple_of(chunk * group, 8), chunk))
-            pltpu.make_async_copy(done.at[where], moved.at[where], sems.at[level, group]).start()
-            return carry
-
-        lax.fori_loop(0, tracer_total // chunk, groups, 0)
-    for level in range(levels):
-        for group in range(tracer_total // chunk):
-            where = (level, slice(None), pl.ds(chunk * group, chunk))
-            pltpu.make_async_copy(done.at[where], moved.at[where], sems.at[level, group]).wait()
+        surface_new[:, lanes] = means[tile, pl.ds(2 * levels, 16, stride=FIELDS), :]
+
+    copies = [
+        pltpu.make_async_copy(winds_new, winds_out, sems.at[levels, 0]),
+        pltpu.make_async_copy(surface_new, surface_out, sems.at[levels, 1]),
+    ]
+    for copy in copies:
+        copy.start()
+
+    strip = split(jnp.concatenate(both_sides(pl.ds(0, base)), axis=1))
+
+    def ghost(edge, place):
+        number = 3 * edge + place
+        picker = remote[number]
+        found = jnp.dot(
+            strip, jnp.concatenate([picker, picker], axis=0), preferred_element_type=jnp.float32
+        )
+        return [
+            near[level, number] + found[level * tracer_total : (level + 1) * tracer_total]
+            for level in range(levels)
+        ]
+
+    def own(cell):
+        return [held[level, cell] for level in range(levels)]
+
+    for cell in CELL_ORDER:
+        row, col = cell // 3, cell % 3
+        west = own(cell - 1) if col > 0 else ghost(3, 2 - row)
+        east = own(cell + 1) if col < 2 else ghost(1, row)
+        south = own(cell - 3) if row > 0 else ghost(0, col)
+        north = own(cell + 3) if row < 2 else ghost(2, 2 - col)
+        for level in range(levels):
+            factor = [factors[pl.ds(16 * cell + at + level, 1), :] for at in (0, 2, 4, 6, 8)]
+            done[level, cell] = (
+                held[level, cell] * factor[4]
+                + (west[level] * factor[0] + east[level] * factor[2])
+                + (south[level] * factor[1] + north[level] * factor[3])
+            )
+            copy = pltpu.make_async_copy(done.at[level, cell], moved.at[level, cell], sems.at[level, cell])
+            copy.start()
+            copies.append(copy)
+    for copy in copies:
+        copy.wait()
 
 
 VMEM = pl.BlockSpec(memory_space=pltpu.VMEM)
@@ -395,7 +410,7 @@
 HBM = pl.BlockSpec(memory_space=pltpu.HBM)
 ANY = pl.BlockSpec(memory_space=pl.ANY)
 LIMIT = pltpu.CompilerParams(vmem_limit_bytes=20 * 1024 * 1024)
-CHUNK = 32
+CELL_ORDER = [4, 1, 3, 5, 7, 0, 2, 6, 8]
 BLOCK = 112
 
 
@@ -415,7 +430,7 @@
     part = pl.pallas_call(
         column_kernel,
         name="column",
-        in_specs=[HBM, HBM, HBM],
+        in_specs=[HBM] * 3,
         out_specs=VMEM,
         out_shape=f32((16, count)),
         scratch_shapes=[
@@ -432,13 +447,14 @@
     for step in range(1, ranks):
         parts.append(lax.ppermute(part, "lev", [(i, i ^ step) for i in range(ranks)]))
 
-    held, inside, outside = pl.pallas_call(
+    held, border, inside, outside = pl.pallas_call(
         strip_kernel,
         name="strips",
-        in_specs=[SMEM, HBM, ANY],
-        out_specs=[VMEM] * 3,
+        in_specs=[VMEM, HBM, ANY],
+        out_specs=[VMEM] * 4,
         out_shape=[
             pltpu.VMEM(turned.shape, jnp.float32),
+            pltpu.VMEM((levels, tracer_total // BLOCK, 8 * BLOCK, 2 * count), jnp.bfloat16),
             pltpu.VMEM(pack_shape, jnp.float32),
             pltpu.VMEM(pack_shape, jnp.float32),
         ],
@@ -446,19 +462,21 @@
         compiler_params=LIMIT,
     )(live_count, in_hbm(turned), part)
 
-    star, inside, outside = pl.pallas_call(
+    ghosts_shape = pltpu.VMEM((levels, 12, tracer_total, count), jnp.float32)
+    star, inside, outside, ghosts = pl.pallas_call(
         star_kernel,
         name="star",
-        in_specs=[SMEM, VMEM] + [VMEM] * (ranks + 4),
-        out_specs=[VMEM] * 3,
+        in_specs=[VMEM, VMEM] + [VMEM] * (ranks + 7),
+        out_specs=[VMEM] * 4,
         out_shape=[
             pltpu.VMEM((2, 16 * FIELDS, 128), jnp.float32),
             pltpu.VMEM(pack_shape, jnp.float32),
             pltpu.VMEM(pack_shape, jnp.float32),
+            ghosts_shape,
         ],
-        input_output_aliases={ranks + 4: 1, ranks + 5: 2},
+        input_output_aliases={ranks + 7: 1, ranks + 8: 2},
         compiler_params=LIMIT,
-    )(live_count, down, *parts, surface, winds, inside, outside)
+    )(live_count, down, *parts, surface, winds, neighbours, rotations, border, inside, outside)
 
     devices = lax.axis_size("elem")
     outside_in = lax.ppermute(
@@ -469,28 +487,30 @@
     sums, ghosts, remote = pl.pallas_call(
         inner_kernel,
         name="inner",
-        in_specs=[VMEM, VMEM, VMEM, VMEM, ANY],
+        in_specs=[VMEM] * 5 + [ANY],
+        input_output_aliases={4: 1},
         out_specs=[VMEM, VMEM, VMEM],
         out_shape=[
             pltpu.VMEM((2, 16 * FIELDS, 128), jnp.float32),
-            pltpu.VMEM((levels, 12, tracer_total, count), jnp.float32),
+            ghosts_shape,
             pltpu.VMEM((12, count, count), jnp.bfloat16),
         ],
         compiler_params=LIMIT,
-    )(neighbours, rotations, star, held, star)
+    )(neighbours, rotations, star, border, ghosts, star)
 
     winds_out, surface_out, moved = pl.pallas_call(
         outer_kernel,
         name="outer",
-        in_specs=[SMEM] + [VMEM] * 8,
-        out_specs=[VMEM, VMEM, HBM],
+        in_specs=[VMEM] + [VMEM] * 8,
+        out_specs=[HBM] * 3,
         out_shape=[f32(winds.shape), f32(surface.shape), f32(turned.shape)],
         scratch_shapes=[
             pltpu.VMEM((2, 16 * FIELDS, 128), jnp.float32),
             pltpu.VMEM((9 * 16, count), jnp.float32),
-            pltpu.VMEM((levels, 12, tracer_total, count), jnp.float32),
+            pltpu.VMEM(winds.shape, jnp.float32),
+            pltpu.VMEM(surface.shape, jnp.float32),
             pltpu.VMEM(turned.shape, jnp.float32),
-            pltpu.SemaphoreType.DMA((levels, tracer_total // CHUNK)),
+            pltpu.SemaphoreType.DMA((levels + 1, 9)),
         ],
         compiler_params=LIMIT,
     )(live_count, neighbours, rotations, sums, held, ghosts, remote, inside_in, outside_in)

time: 30 us -> 27.2 us (0.907)
  starting transfers between devices: 12.7 us -> 10.4 us
  Pallas kernels: 15.7 us -> 14.5 us
  waiting for transfers between devices: 0.01 us -> 0.53 us
    ppermute x1, starting transfers between devices: 8.41 us -> 6.16 us  [body(): lax.ppermute(outside, 'elem', [(i, (((i + 1) % devices ^ 1) - 1) % device...]
    pallas_call x5, Pallas kernels: 15.7 us -> 14.5 us  [the longest x1 4.57 us: body(): pl.pallas_call(outer_kernel, name='outer', in_specs=[VMEM] + [VMEM] * 8,...]
    ppermute x1, waiting for transfers between devices: 0.01 us -> 0.52 us  [body(): lax.ppermute(outside, 'elem', [(i, (((i + 1) % devices ^ 1) - 1) % device...]
  transfers between devices with their start and end apart: 5 -> 5, of which waited for: 0 -> 1; matrix products, arithmetic and copies ran while one was open for 0% -> 0% of each run, Pallas kernels for 31% -> 23%
where the time goes in v2:
time: 27.2 us; the launch traced here: 27.1 us
  Pallas kernels  14.5 us (53%)
  starting transfers between devices  10.4 us (38%)
  between operations  1.6 us (6%)
  waiting for transfers between devices  0.53 us (2%)
    ppermute x1, starting transfers between devices, body(): lax.ppermute(outside, 'elem', [(i, (((i + 1) % devices ^ 1) - 1) % device...  6.16 us
    pallas_call x1, Pallas kernels, body(): pl.pallas_call(outer_kernel, name='outer', in_specs=[VMEM] + [VMEM] * 8,...  4.57 us
    ppermute x3, starting transfers between devices, body(): lax.ppermute(part, 'lev', [(i, i ^ step) for i in range(ranks)])  4.18 us
    pallas_call x1, Pallas kernels, body(): pl.pallas_call(inner_kernel, name='inner', in_specs=[VMEM] * 5 + [ANY], i...  3.25 us
    pallas_call x1, Pallas kernels, body(): pl.pallas_call(strip_kernel, name='strips', in_specs=[VMEM, HBM, ANY], ou...  3.1 us
    pallas_call x1, Pallas kernels, body(): pl.pallas_call(star_kernel, name='star', in_specs=[VMEM, VMEM] + [VMEM] *...  2.51 us
    pallas_call x1, Pallas kernels, body(): pl.pallas_call(column_kernel, name='column', in_specs=[HBM] * 3, out_spec...  1.07 us
  transfers between devices with their start and end apart: 5, of which 1 were waited for; matrix products, arithmetic and copies ran while one was open for 0% of the time, Pallas kernels for 23%

profile of v2, /device:TPU:4, one launch (start us, length us, event | category | flops | bytes accessed | tf_op | source)
XLA Modules:
  0.0 27.1 jit_solution(5160168822800837830)
XLA Ops:
  0.6 0.0 copy-start.4
  0.6 0.0 copy-start
  0.7 0.0 copy-start.2
  0.7 0.0 copy-start.1
  0.7 0.0 copy-start.3
  0.7 1.1 %column.1.order.refs_0_ = f32[16,256]{1,0:T(8,128)S(1)} custom-call(f32[2]{0:T(128)} %thickness_in.1, f32[16,32]{1,0:T(8,128)} %constant.4.clone.matrix_in, f32[2,2,16,256]{3,2,1,0:T(8,128)} %refs_5_.1), custom_call_target="tpu_custom_call" | custom-call | tf_op jit(solution)/shard_map/column/pallas_call | solution.py:430
  1.8 0.6 %collective-permute-start.2 = (f32[16,256]{1,0:T(8,128)S(1)}, f32[16,256]{1,0:T(8,128)S(1)}, u32[]{:S(2)}, u32[]{:S(2)}) collective-permute-start(f32[16,256]{1,0:T(8,128)S(1)} %column.1.order.refs_0_), channel_id=1, source_target_pairs={{0,3},{1,2},{2,1},{3,0},{4,7},{5,6},{6,5},{7,4},{8,11},{9,10},{10,... | collective-permute-start | bytes 49160 | tf_op jit(solution)/shard_map/ppermute | solution.py:448
  2.4 2.7 %collective-permute-start.1 = (f32[16,256]{1,0:T(8,128)S(1)}, f32[16,256]{1,0:T(8,128)S(1)}, u32[]{:S(2)}, u32[]{:S(2)}) collective-permute-start(f32[16,256]{1,0:T(8,128)S(1)} %column.1.order.refs_0_), channel_id=1, source_target_pairs={{0,2},{1,3},{2,0},{3,1},{4,6},{5,7},{6,4},{7,5},{8,10},{9,11},{10,... | collective-permute-start | bytes 49160 | tf_op jit(solution)/shard_map/ppermute | solution.py:448
  5.1 0.8 %collective-permute-start = (f32[16,256]{1,0:T(8,128)S(1)}, f32[16,256]{1,0:T(8,128)S(1)}, u32[]{:S(2)}, u32[]{:S(2)}) collective-permute-start(f32[16,256]{1,0:T(8,128)S(1)} %column.1.order.refs_0_), channel_id=1, source_target_pairs={{0,1},{1,0},{2,3},{3,2},{4,5},{5,4},{6,7},{7,6},{8,9},{9,8},{10,11... | collective-permute-start | bytes 49160 | tf_op jit(solution)/shard_map/ppermute | solution.py:448
  6.6 3.1 %strips.1 = (f32[2,9,224,256]{3,2,1,0:T(8,128)S(1)}, bf16[2,2,896,512]{3,2,1,0:T(8,128)(2,1)S(1)}, f32[464,128]{1,0:T(8,128)S(1)}, f32[464,128]{1,0:T(8,128)S(1)}) custom-call(s32[1]{0:T(128)S(6)} %copy.18.live, f32[2,9,224,256]{3,2,1,0:T(8,128)} %bitcast.2, f32[16,256]{1,0:T(8,128)S(1)} %column.1.order.refs_0_), custom_call_target="tpu_custom_call" | custom-call | tf_op jit(solution)/shard_map/strips/pallas_call | solution.py:450
  9.7 0.0 collective-permute-done.2.refs_3_
  9.7 0.0 collective-permute-done.1.refs_2_
  9.7 0.0 collective-permute-done.refs_1_
  9.7 0.0 copy-done.4
  9.7 0.0 copy-done
  9.7 0.0 copy-done.2
  9.8 0.0 copy-done.1
  9.8 0.0 copy-done.3
  9.8 2.5 %star.1 = (f32[2,128,128]{2,1,0:T(8,128)S(1)}, f32[464,128]{1,0:T(8,128)S(1)}, f32[464,128]{1,0:T(8,128)S(1)}, f32[2,12,224,256]{3,2,1,0:T(8,128)S(1)}) custom-call(s32[1]{0:T(128)S(6)} %copy.18.live, f32[32,16]{1,0:T(8,128)S(1)} %copy-done.4, f32[16,256]{1,0:T(8,128)S(1)} %column.1.order.refs_0_, ...), custom_call_target="tpu_custom_call", output_to_operand_aliasing={{1}: (11, {}), {2}: (12, {})} | custom-call | tf_op jit(solution)/shard_map/star/pallas_call | solution.py:466
  12.3 0.1 collective-permute-start.3
  12.4 6.2 %collective-permute-start.4 = (f32[464,128]{1,0:T(8,128)S(1)}, f32[464,128]{1,0:T(8,128)S(1)}, u32[]{:S(2)}, u32[]{:S(2)}) collective-permute-start(f32[464,128]{1,0:T(8,128)S(1)} %get-tuple-element.27), channel_id=1, source_target_pairs={{0,252},{4,8},{8,4},{12,16},{16,12},{20,24},{24,20},{28,32},{32,28... | collective-permute-start | bytes 712712 | tf_op jit(solution)/shard_map/ppermute | solution.py:482
  18.6 3.3 %inner.1 = (f32[2,128,128]{2,1,0:T(8,128)S(1)}, f32[2,12,224,256]{3,2,1,0:T(8,128)S(1)}, bf16[12,256,256]{2,1,0:T(8,128)(2,1)S(1)}) custom-call(s32[4,256]{1,0:T(4,128)S(1)} %copy-done.1, s32[4,256]{1,0:T(4,128)S(1)} %copy-done.2, f32[2,128,128]{2,1,0:T(8,128)S(1)} %get-tuple-element.20.star.order, ...), custom_call_target="tpu_custom_call", output_to_operand_aliasing={{1}: (4, {})} | custom-call | tf_op jit(solution)/shard_map/inner/pallas_call | solution.py:487
  21.8 0.0 collective-permute-done.3.inside
  21.8 0.5 %collective-permute-done.4.outside = f32[464,128]{1,0:T(8,128)S(1)} collective-permute-done((f32[464,128]{1,0:T(8,128)S(1)}, f32[464,128]{1,0:T(8,128)S(1)}, u32[]{:S(2)}, u32[]{:S(2)}) %collective-permute-start.4) | collective-permute-done | bytes 237600 | tf_op jit(solution)/shard_map/ppermute | solution.py:482
  22.3 4.6 %outer.1 = (f32[2,2,16,256]{3,2,1,0:T(8,128)}, f32[16,256]{1,0:T(8,128)}, f32[2,9,224,256]{3,2,1,0:T(8,128)}) custom-call(s32[1]{0:T(128)S(6)} %copy.18.live, s32[4,256]{1,0:T(4,128)S(1)} %copy-done.1, s32[4,256]{1,0:T(4,128)S(1)} %copy-done.2, f32[2,128,128]{2,1,0:T(8,128)S(1)} %get-tuple-element.22.sums, f32[2,9,224,256]{3,2,1,0:T(8,128)S(1)} %get-tuple-element.23.held, ...), custom_call_target="tpu_custom_call" | custom-call | tf_op jit(solution)/shard_map/outer/pallas_call | solution.py:501
Async XLA Ops:
  0.6 9.1 %copy-start.4 = (f32[32,16]{1,0:T(8,128)S(1)}, f32[32,16]{1,0:T(8,128)}, u32[]{:S(2)}) copy-start(f32[32,16]{1,0:T(8,128)} %constant.5.clone.matrix) | copy-start | bytes 6148
  0.6 9.1 %copy-start = (f32[2,2,16,256]{3,2,1,0:T(8,128)S(1)}, f32[2,2,16,256]{3,2,1,0:T(8,128)}, u32[]{:S(2)}) copy-start(f32[2,2,16,256]{3,2,1,0:T(8,128)} %refs_5_.1) | copy-start | bytes 196612
  0.7 9.1 %copy-start.2 = (s32[4,256]{1,0:T(4,128)S(1)}, s32[4,256]{1,0:T(4,128)}, u32[]{:S(2)}) copy-start(s32[4,256]{1,0:T(4,128)} %rotations.3) | copy-start | bytes 12292
  0.7 9.1 %copy-start.1 = (s32[4,256]{1,0:T(4,128)S(1)}, s32[4,256]{1,0:T(4,128)}, u32[]{:S(2)}) copy-start(s32[4,256]{1,0:T(4,128)} %neighbours.3) | copy-start | bytes 12292
  0.7 9.1 %copy-start.3 = (f32[16,256]{1,0:T(8,128)S(1)}, f32[16,256]{1,0:T(8,128)}, u32[]{:S(2)}) copy-start(f32[16,256]{1,0:T(8,128)} %refs_4_.1) | copy-start | bytes 49156
  1.8 7.9 %collective-permute-start.2 = (f32[16,256]{1,0:T(8,128)S(1)}, f32[16,256]{1,0:T(8,128)S(1)}, u32[]{:S(2)}, u32[]{:S(2)}) collective-permute-start(f32[16,256]{1,0:T(8,128)S(1)} %column.1.order.refs_0_), channel_id=1, source_target_pairs={{0,3},{1,2},{2,1},{3,0},{4,7},{5,6},{6,5},{7,4},{8,11},{9,10},{10,... | collective-permute-start | bytes 49160 | tf_op jit(solution)/shard_map/ppermute | solution.py:448
  2.4 7.3 %collective-permute-start.1 = (f32[16,256]{1,0:T(8,128)S(1)}, f32[16,256]{1,0:T(8,128)S(1)}, u32[]{:S(2)}, u32[]{:S(2)}) collective-permute-start(f32[16,256]{1,0:T(8,128)S(1)} %column.1.order.refs_0_), channel_id=1, source_target_pairs={{0,2},{1,3},{2,0},{3,1},{4,6},{5,7},{6,4},{7,5},{8,10},{9,11},{10,... | collective-permute-start | bytes 49160 | tf_op jit(solution)/shard_map/ppermute | solution.py:448
  5.1 4.6 %collective-permute-start = (f32[16,256]{1,0:T(8,128)S(1)}, f32[16,256]{1,0:T(8,128)S(1)}, u32[]{:S(2)}, u32[]{:S(2)}) collective-permute-start(f32[16,256]{1,0:T(8,128)S(1)} %column.1.order.refs_0_), channel_id=1, source_target_pairs={{0,1},{1,0},{2,3},{3,2},{4,5},{5,4},{6,7},{7,6},{8,9},{9,8},{10,11... | collective-permute-start | bytes 49160 | tf_op jit(solution)/shard_map/ppermute | solution.py:448
  12.3 9.5 %collective-permute-start.3 = (f32[464,128]{1,0:T(8,128)S(1)}, f32[464,128]{1,0:T(8,128)S(1)}, u32[]{:S(2)}, u32[]{:S(2)}) collective-permute-start(f32[464,128]{1,0:T(8,128)S(1)} %get-tuple-element.26), channel_id=1, source_target_pairs={{0,4},{4,0},{8,12},{12,8},{16,20},{20,16},{24,28},{28,24},{32,36},... | collective-permute-start | bytes 712712 | tf_op jit(solution)/shard_map/ppermute | solution.py:485
  12.4 9.9 %collective-permute-start.4 = (f32[464,128]{1,0:T(8,128)S(1)}, f32[464,128]{1,0:T(8,128)S(1)}, u32[]{:S(2)}, u32[]{:S(2)}) collective-permute-start(f32[464,128]{1,0:T(8,128)S(1)} %get-tuple-element.27), channel_id=1, source_target_pairs={{0,252},{4,8},{8,4},{12,16},{16,12},{20,24},{24,20},{28,32},{32,28... | collective-permute-start | bytes 712712 | tf_op jit(solution)/shard_map/ppermute | solution.py:482

commit v3 on v2

--- a/solution.py
+++ b/solution.py
@@ -163,9 +163,15 @@
                 packed = moved if packed is None else jnp.where(lane_block == place, moved, packed)
             target[pl.ds(base + FIELDS * block, FIELDS), :] = packed
 
-    @pl.when(lax.axis_index("elem") == 0)
+    me = lax.axis_index("elem")
+
+    @pl.when(me == 0)
     def _():
         near_ghosts(neighbours, rotations, border, ghosts, range(1))
+
+    @pl.when(me == 1)
+    def _():
+        near_ghosts(neighbours, rotations, border, ghosts, range(levels))
 
 
 def add_edges(nodes, codes, ring):
@@ -287,11 +293,13 @@
         for edge in range(4):
             remote[3 * edge + place] = picks(line, source[edge : edge + 1])
 
-    @pl.when(me != 0)
+    @pl.when(me > 1)
     def _():
         near_ghosts(neighbours, rotations, border, ghosts, range(1))
 
-    near_ghosts(neighbours, rotations, border, ghosts, range(1, levels))
+    @pl.when(me != 1)
+    def _():
+        near_ghosts(neighbours, rotations, border, ghosts, range(1, levels))
 
 
 def outer_kernel(
@@ -302,8 +310,8 @@
     held,
     near,
     remote,
+    outside,
     inside,
-    outside,
     winds_out,
     surface_out,
     moved,
@@ -513,7 +521,7 @@
             pltpu.SemaphoreType.DMA((levels + 1, 9)),
         ],
         compiler_params=LIMIT,
-    )(live_count, neighbours, rotations, sums, held, ghosts, remote, inside_in, outside_in)
+    )(live_count, neighbours, rotations, sums, held, ghosts, remote, outside_in, inside_in)
     return winds_out, surface_out, jnp.transpose(moved, (0, 1, 3, 2))
 
 

time: 27.2 us -> 26.4 us (0.971); the launches traced: 27.1 us -> 26 us
  starting transfers between devices: 10.4 us -> 8.93 us
  waiting for transfers between devices: 0.53 us -> 0.94 us
    ppermute x1, starting transfers between devices: 6.16 us -> 4.75 us  [body(): lax.ppermute(outside, 'elem', [(i, (((i + 1) % devices ^ 1) - 1) % device...]
    ppermute x1, waiting for transfers between devices: 0.52 us -> 0.92 us  [body(): lax.ppermute(outside, 'elem', [(i, (((i + 1) % devices ^ 1) - 1) % device...]
  transfers between devices with their start and end apart: 5 -> 5, of which waited for: 1 -> 1; matrix products, arithmetic and copies ran while one was open for 0% -> 0% of each run, Pallas kernels for 23% -> 24%
where the time goes in v3:
time: 26.4 us; the launch traced here: 26 us
  Pallas kernels  14.5 us (55%)
  starting transfers between devices  8.93 us (34%)
  between operations  1.58 us (6%)
  waiting for transfers between devices  0.94 us (4%)
    ppermute x1, starting transfers between devices, body(): lax.ppermute(outside, 'elem', [(i, (((i + 1) % devices ^ 1) - 1) % device...  4.75 us
    pallas_call x1, Pallas kernels, body(): pl.pallas_call(outer_kernel, name='outer', in_specs=[VMEM] + [VMEM] * 8,...  4.57 us
    ppermute x3, starting transfers between devices, body(): lax.ppermute(part, 'lev', [(i, i ^ step) for i in range(ranks)])  4.18 us
    pallas_call x1, Pallas kernels, body(): pl.pallas_call(inner_kernel, name='inner', in_specs=[VMEM] * 5 + [ANY], i...  3.25 us
    pallas_call x1, Pallas kernels, body(): pl.pallas_call(strip_kernel, name='strips', in_specs=[VMEM, HBM, ANY], ou...  3.1 us
    pallas_call x1, Pallas kernels, body(): pl.pallas_call(star_kernel, name='star', in_specs=[VMEM, VMEM] + [VMEM] *...  2.52 us
    pallas_call x1, Pallas kernels, body(): pl.pallas_call(column_kernel, name='column', in_specs=[HBM] * 3, out_spec...  1.07 us
    ppermute x1, waiting for transfers between devices, body(): lax.ppermute(outside, 'elem', [(i, (((i + 1) % devices ^ 1) - 1) % device...  0.92 us
  transfers between devices with their start and end apart: 5, of which 1 were waited for; matrix products, arithmetic and copies ran while one was open for 0% of the time, Pallas kernels for 24%

profile of v3, /device:TPU:4, one launch (start us, length us, event | category | flops | bytes accessed | tf_op | source)
XLA Modules:
  0.0 26.0 jit_solution(13475017006258032725)
XLA Ops:
  0.6 0.0 copy-start.4
  0.6 0.0 copy-start
  0.7 0.0 copy-start.2
  0.7 0.0 copy-start.1
  0.7 0.0 copy-start.3
  0.7 1.1 %column.1.order.refs_0_ = f32[16,256]{1,0:T(8,128)S(1)} custom-call(f32[2]{0:T(128)} %thickness_in.1, f32[16,32]{1,0:T(8,128)} %constant.4.clone.matrix_in, f32[2,2,16,256]{3,2,1,0:T(8,128)} %refs_5_.1), custom_call_target="tpu_custom_call" | custom-call | tf_op jit(solution)/shard_map/column/pallas_call | solution.py:438
  1.8 0.6 %collective-permute-start.2 = (f32[16,256]{1,0:T(8,128)S(1)}, f32[16,256]{1,0:T(8,128)S(1)}, u32[]{:S(2)}, u32[]{:S(2)}) collective-permute-start(f32[16,256]{1,0:T(8,128)S(1)} %column.1.order.refs_0_), channel_id=1, source_target_pairs={{0,3},{1,2},{2,1},{3,0},{4,7},{5,6},{6,5},{7,4},{8,11},{9,10},{10,... | collective-permute-start | bytes 49160 | tf_op jit(solution)/shard_map/ppermute | solution.py:456
  2.4 2.7 %collective-permute-start.1 = (f32[16,256]{1,0:T(8,128)S(1)}, f32[16,256]{1,0:T(8,128)S(1)}, u32[]{:S(2)}, u32[]{:S(2)}) collective-permute-start(f32[16,256]{1,0:T(8,128)S(1)} %column.1.order.refs_0_), channel_id=1, source_target_pairs={{0,2},{1,3},{2,0},{3,1},{4,6},{5,7},{6,4},{7,5},{8,10},{9,11},{10,... | collective-permute-start | bytes 49160 | tf_op jit(solution)/shard_map/ppermute | solution.py:456
  5.1 0.8 %collective-permute-start = (f32[16,256]{1,0:T(8,128)S(1)}, f32[16,256]{1,0:T(8,128)S(1)}, u32[]{:S(2)}, u32[]{:S(2)}) collective-permute-start(f32[16,256]{1,0:T(8,128)S(1)} %column.1.order.refs_0_), channel_id=1, source_target_pairs={{0,1},{1,0},{2,3},{3,2},{4,5},{5,4},{6,7},{7,6},{8,9},{9,8},{10,11... | collective-permute-start | bytes 49160 | tf_op jit(solution)/shard_map/ppermute | solution.py:456
  6.6 3.1 %strips.1 = (f32[2,9,224,256]{3,2,1,0:T(8,128)S(1)}, bf16[2,2,896,512]{3,2,1,0:T(8,128)(2,1)S(1)}, f32[464,128]{1,0:T(8,128)S(1)}, f32[464,128]{1,0:T(8,128)S(1)}) custom-call(s32[1]{0:T(128)S(6)} %copy.18.live, f32[2,9,224,256]{3,2,1,0:T(8,128)} %bitcast.2, f32[16,256]{1,0:T(8,128)S(1)} %column.1.order.refs_0_), custom_call_target="tpu_custom_call" | custom-call | tf_op jit(solution)/shard_map/strips/pallas_call | solution.py:458
  9.7 0.0 collective-permute-done.2.refs_3_
  9.7 0.0 collective-permute-done.1.refs_2_
  9.7 0.0 collective-permute-done.refs_1_
  9.7 0.0 copy-done.4
  9.7 0.0 copy-done
  9.7 0.0 copy-done.2
  9.8 0.0 copy-done.1
  9.8 0.0 copy-done.3
  9.8 2.5 %star.1 = (f32[2,128,128]{2,1,0:T(8,128)S(1)}, f32[464,128]{1,0:T(8,128)S(1)}, f32[464,128]{1,0:T(8,128)S(1)}, f32[2,12,224,256]{3,2,1,0:T(8,128)S(1)}) custom-call(s32[1]{0:T(128)S(6)} %copy.18.live, f32[32,16]{1,0:T(8,128)S(1)} %copy-done.4, f32[16,256]{1,0:T(8,128)S(1)} %column.1.order.refs_0_, ...), custom_call_target="tpu_custom_call", output_to_operand_aliasing={{1}: (11, {}), {2}: (12, {})} | custom-call | tf_op jit(solution)/shard_map/star/pallas_call | solution.py:474
  12.3 4.8 %collective-permute-start.3 = (f32[464,128]{1,0:T(8,128)S(1)}, f32[464,128]{1,0:T(8,128)S(1)}, u32[]{:S(2)}, u32[]{:S(2)}) collective-permute-start(f32[464,128]{1,0:T(8,128)S(1)} %get-tuple-element.26), channel_id=1, source_target_pairs={{0,252},{4,8},{8,4},{12,16},{16,12},{20,24},{24,20},{28,32},{32,28... | collective-permute-start | bytes 712712 | tf_op jit(solution)/shard_map/ppermute | solution.py:490
  17.1 0.0 collective-permute-start.4
  17.1 3.3 %inner.1 = (f32[2,128,128]{2,1,0:T(8,128)S(1)}, f32[2,12,224,256]{3,2,1,0:T(8,128)S(1)}, bf16[12,256,256]{2,1,0:T(8,128)(2,1)S(1)}) custom-call(s32[4,256]{1,0:T(4,128)S(1)} %copy-done.1, s32[4,256]{1,0:T(4,128)S(1)} %copy-done.2, f32[2,128,128]{2,1,0:T(8,128)S(1)} %get-tuple-element.20.star.order, ...), custom_call_target="tpu_custom_call", output_to_operand_aliasing={{1}: (4, {})} | custom-call | tf_op jit(solution)/shard_map/inner/pallas_call | solution.py:495
  20.3 0.9 %collective-permute-done.3.outside = f32[464,128]{1,0:T(8,128)S(1)} collective-permute-done((f32[464,128]{1,0:T(8,128)S(1)}, f32[464,128]{1,0:T(8,128)S(1)}, u32[]{:S(2)}, u32[]{:S(2)}) %collective-permute-start.3) | collective-permute-done | bytes 237600 | tf_op jit(solution)/shard_map/ppermute | solution.py:490
  21.2 0.0 collective-permute-done.4.inside
  21.2 4.6 %outer.1 = (f32[2,2,16,256]{3,2,1,0:T(8,128)}, f32[16,256]{1,0:T(8,128)}, f32[2,9,224,256]{3,2,1,0:T(8,128)}) custom-call(s32[1]{0:T(128)S(6)} %copy.18.live, s32[4,256]{1,0:T(4,128)S(1)} %copy-done.1, s32[4,256]{1,0:T(4,128)S(1)} %copy-done.2, f32[2,128,128]{2,1,0:T(8,128)S(1)} %get-tuple-element.22.sums, f32[2,9,224,256]{3,2,1,0:T(8,128)S(1)} %get-tuple-element.23.held, ...), custom_call_target="tpu_custom_call" | custom-call | tf_op jit(solution)/shard_map/outer/pallas_call | solution.py:509
Async XLA Ops:
  0.6 9.1 %copy-start.4 = (f32[32,16]{1,0:T(8,128)S(1)}, f32[32,16]{1,0:T(8,128)}, u32[]{:S(2)}) copy-start(f32[32,16]{1,0:T(8,128)} %constant.5.clone.matrix) | copy-start | bytes 6148
  0.6 9.1 %copy-start = (f32[2,2,16,256]{3,2,1,0:T(8,128)S(1)}, f32[2,2,16,256]{3,2,1,0:T(8,128)}, u32[]{:S(2)}) copy-start(f32[2,2,16,256]{3,2,1,0:T(8,128)} %refs_5_.1) | copy-start | bytes 196612
  0.7 9.1 %copy-start.2 = (s32[4,256]{1,0:T(4,128)S(1)}, s32[4,256]{1,0:T(4,128)}, u32[]{:S(2)}) copy-start(s32[4,256]{1,0:T(4,128)} %rotations.3) | copy-start | bytes 12292
  0.7 9.1 %copy-start.1 = (s32[4,256]{1,0:T(4,128)S(1)}, s32[4,256]{1,0:T(4,128)}, u32[]{:S(2)}) copy-start(s32[4,256]{1,0:T(4,128)} %neighbours.3) | copy-start | bytes 12292
  0.7 9.1 %copy-start.3 = (f32[16,256]{1,0:T(8,128)S(1)}, f32[16,256]{1,0:T(8,128)}, u32[]{:S(2)}) copy-start(f32[16,256]{1,0:T(8,128)} %refs_4_.1) | copy-start | bytes 49156
  1.8 7.9 %collective-permute-start.2 = (f32[16,256]{1,0:T(8,128)S(1)}, f32[16,256]{1,0:T(8,128)S(1)}, u32[]{:S(2)}, u32[]{:S(2)}) collective-permute-start(f32[16,256]{1,0:T(8,128)S(1)} %column.1.order.refs_0_), channel_id=1, source_target_pairs={{0,3},{1,2},{2,1},{3,0},{4,7},{5,6},{6,5},{7,4},{8,11},{9,10},{10,... | collective-permute-start | bytes 49160 | tf_op jit(solution)/shard_map/ppermute | solution.py:456
  2.4 7.3 %collective-permute-start.1 = (f32[16,256]{1,0:T(8,128)S(1)}, f32[16,256]{1,0:T(8,128)S(1)}, u32[]{:S(2)}, u32[]{:S(2)}) collective-permute-start(f32[16,256]{1,0:T(8,128)S(1)} %column.1.order.refs_0_), channel_id=1, source_target_pairs={{0,2},{1,3},{2,0},{3,1},{4,6},{5,7},{6,4},{7,5},{8,10},{9,11},{10,... | collective-permute-start | bytes 49160 | tf_op jit(solution)/shard_map/ppermute | solution.py:456
  5.1 4.6 %collective-permute-start = (f32[16,256]{1,0:T(8,128)S(1)}, f32[16,256]{1,0:T(8,128)S(1)}, u32[]{:S(2)}, u32[]{:S(2)}) collective-permute-start(f32[16,256]{1,0:T(8,128)S(1)} %column.1.order.refs_0_), channel_id=1, source_target_pairs={{0,1},{1,0},{2,3},{3,2},{4,5},{5,4},{6,7},{7,6},{8,9},{9,8},{10,11... | collective-permute-start | bytes 49160 | tf_op jit(solution)/shard_map/ppermute | solution.py:456
  12.3 8.9 %collective-permute-start.3 = (f32[464,128]{1,0:T(8,128)S(1)}, f32[464,128]{1,0:T(8,128)S(1)}, u32[]{:S(2)}, u32[]{:S(2)}) collective-permute-start(f32[464,128]{1,0:T(8,128)S(1)} %get-tuple-element.26), channel_id=1, source_target_pairs={{0,252},{4,8},{8,4},{12,16},{16,12},{20,24},{24,20},{28,32},{32,28... | collective-permute-start | bytes 712712 | tf_op jit(solution)/shard_map/ppermute | solution.py:490
  17.1 4.2 %collective-permute-start.4 = (f32[464,128]{1,0:T(8,128)S(1)}, f32[464,128]{1,0:T(8,128)S(1)}, u32[]{:S(2)}, u32[]{:S(2)}) collective-permute-start(f32[464,128]{1,0:T(8,128)S(1)} %get-tuple-element.27), channel_id=1, source_target_pairs={{0,4},{4,0},{8,12},{12,8},{16,20},{20,16},{24,28},{28,24},{32,36},... | collective-permute-start | bytes 712712 | tf_op jit(solution)/shard_map/ppermute | solution.py:493

commit v4 on v3

--- a/solution.py
+++ b/solution.py
@@ -104,12 +104,14 @@
 def strip_kernel(live, tracers, order, held, border, inside, outside, sems):
     del order
     levels, _, tracer_total, count = tracers.shape
-    loads = [
-        pltpu.make_async_copy(tracers.at[level], held.at[level], sems.at[level])
-        for level in range(levels)
-    ]
-    for load in loads:
-        load.start()
+    loads = {}
+    for level in range(levels):
+        for block in range(tracer_total // BLOCK):
+            where = (level, slice(None), pl.ds(BLOCK * block, BLOCK))
+            loads[level, block] = pltpu.make_async_copy(
+                tracers.at[where], held.at[where], sems.at[level, block]
+            )
+            loads[level, block].start()
     line = lax.broadcasted_iota(jnp.int32, (count, 256), 0)
     lane = lax.broadcasted_iota(jnp.int32, (count, 256), 1)
     starts = [128 * tile + at for tile, at in strips(live)]
@@ -117,8 +119,8 @@
     picker = jnp.concatenate([picker, picker], axis=0)
     part = (lax.broadcasted_iota(jnp.int32, (BLOCK, 256), 1) % 128) // HALO
     for level in range(levels):
-        loads[level].wait()
         for block in range(tracer_total // BLOCK):
+            loads[level, block].wait()
             rows = pl.ds(BLOCK * block, BLOCK)
             for place, cell in enumerate(CELL_RING):
                 border[level, block, pl.ds(BLOCK * place, BLOCK), :] = split(held[level, cell, rows, :])
@@ -466,7 +468,7 @@
             pltpu.VMEM(pack_shape, jnp.float32),
             pltpu.VMEM(pack_shape, jnp.float32),
         ],
-        scratch_shapes=[pltpu.SemaphoreType.DMA((levels,))],
+        scratch_shapes=[pltpu.SemaphoreType.DMA((levels, tracer_total // BLOCK))],
         compiler_params=LIMIT,
     )(live_count, in_hbm(turned), part)
 

time: 26.4 us -> 27.1 us (1.027)
  Pallas kernels: 14.5 us -> 15.2 us
    pallas_call x1, Pallas kernels: 3.1 us -> 3.81 us  [body(): pl.pallas_call(strip_kernel, name='strips', in_specs=[VMEM, HBM, ANY], ou...]
  transfers between devices with their start and end apart: 5 -> 5, of which waited for: 1 -> 1; matrix products, arithmetic and copies ran while one was open for 0% -> 0% of each run, Pallas kernels for 24% -> 26%
where the time goes in v4:
time: 27.1 us; the launch traced here: 26.7 us
  Pallas kernels  15.2 us (56%)
  starting transfers between devices  8.93 us (33%)
  between operations  1.58 us (6%)
  waiting for transfers between devices  0.93 us (3%)
    ppermute x1, starting transfers between devices, body(): lax.ppermute(outside, 'elem', [(i, (((i + 1) % devices ^ 1) - 1) % device...  4.75 us
    pallas_call x1, Pallas kernels, body(): pl.pallas_call(outer_kernel, name='outer', in_specs=[VMEM] + [VMEM] * 8,...  4.58 us
    ppermute x3, starting transfers between devices, body(): lax.ppermute(part, 'lev', [(i, i ^ step) for i in range(ranks)])  4.18 us
    pallas_call x1, Pallas kernels, body(): pl.pallas_call(strip_kernel, name='strips', in_specs=[VMEM, HBM, ANY], ou...  3.81 us
    pallas_call x1, Pallas kernels, body(): pl.pallas_call(inner_kernel, name='inner', in_specs=[VMEM] * 5 + [ANY], i...  3.26 us
    pallas_call x1, Pallas kernels, body(): pl.pallas_call(star_kernel, name='star', in_specs=[VMEM, VMEM] + [VMEM] *...  2.52 us
    pallas_call x1, Pallas kernels, body(): pl.pallas_call(column_kernel, name='column', in_specs=[HBM] * 3, out_spec...  1.07 us
    ppermute x1, waiting for transfers between devices, body(): lax.ppermute(outside, 'elem', [(i, (((i + 1) % devices ^ 1) - 1) % device...  0.92 us
  transfers between devices with their start and end apart: 5, of which 1 were waited for; matrix products, arithmetic and copies ran while one was open for 0% of the time, Pallas kernels for 26%

profile of v4, /device:TPU:4, one launch (start us, length us, event | category | flops | bytes accessed | tf_op | source)
XLA Modules:
  0.0 26.7 jit_solution(13954125782668829928)
XLA Ops:
  0.6 0.0 copy-start.4
  0.6 0.0 copy-start
  0.7 0.0 copy-start.2
  0.7 0.0 copy-start.1
  0.7 0.0 copy-start.3
  0.7 1.1 %column.1.order.refs_0_ = f32[16,256]{1,0:T(8,128)S(1)} custom-call(f32[2]{0:T(128)} %thickness_in.1, f32[16,32]{1,0:T(8,128)} %constant.4.clone.matrix_in, f32[2,2,16,256]{3,2,1,0:T(8,128)} %refs_5_.1), custom_call_target="tpu_custom_call" | custom-call | tf_op jit(solution)/shard_map/column/pallas_call | solution.py:440
  1.8 0.6 %collective-permute-start.2 = (f32[16,256]{1,0:T(8,128)S(1)}, f32[16,256]{1,0:T(8,128)S(1)}, u32[]{:S(2)}, u32[]{:S(2)}) collective-permute-start(f32[16,256]{1,0:T(8,128)S(1)} %column.1.order.refs_0_), channel_id=1, source_target_pairs={{0,3},{1,2},{2,1},{3,0},{4,7},{5,6},{6,5},{7,4},{8,11},{9,10},{10,... | collective-permute-start | bytes 49160 | tf_op jit(solution)/shard_map/ppermute | solution.py:458
  2.4 2.7 %collective-permute-start.1 = (f32[16,256]{1,0:T(8,128)S(1)}, f32[16,256]{1,0:T(8,128)S(1)}, u32[]{:S(2)}, u32[]{:S(2)}) collective-permute-start(f32[16,256]{1,0:T(8,128)S(1)} %column.1.order.refs_0_), channel_id=1, source_target_pairs={{0,2},{1,3},{2,0},{3,1},{4,6},{5,7},{6,4},{7,5},{8,10},{9,11},{10,... | collective-permute-start | bytes 49160 | tf_op jit(solution)/shard_map/ppermute | solution.py:458
  5.1 0.8 %collective-permute-start = (f32[16,256]{1,0:T(8,128)S(1)}, f32[16,256]{1,0:T(8,128)S(1)}, u32[]{:S(2)}, u32[]{:S(2)}) collective-permute-start(f32[16,256]{1,0:T(8,128)S(1)} %column.1.order.refs_0_), channel_id=1, source_target_pairs={{0,1},{1,0},{2,3},{3,2},{4,5},{5,4},{6,7},{7,6},{8,9},{9,8},{10,11... | collective-permute-start | bytes 49160 | tf_op jit(solution)/shard_map/ppermute | solution.py:458
  6.6 3.8 %strips.1 = (f32[2,9,224,256]{3,2,1,0:T(8,128)S(1)}, bf16[2,2,896,512]{3,2,1,0:T(8,128)(2,1)S(1)}, f32[464,128]{1,0:T(8,128)S(1)}, f32[464,128]{1,0:T(8,128)S(1)}) custom-call(s32[1]{0:T(128)S(6)} %copy.18.live, f32[2,9,224,256]{3,2,1,0:T(8,128)} %bitcast.2, f32[16,256]{1,0:T(8,128)S(1)} %column.1.order.refs_0_), custom_call_target="tpu_custom_call" | custom-call | tf_op jit(solution)/shard_map/strips/pallas_call | solution.py:460
  10.4 0.0 collective-permute-done.2.refs_3_
  10.4 0.0 collective-permute-done.1.refs_2_
  10.4 0.0 collective-permute-done.refs_1_
  10.4 0.0 copy-done.4
  10.4 0.0 copy-done
  10.5 0.0 copy-done.2
  10.5 0.0 copy-done.1
  10.5 0.0 copy-done.3
  10.5 2.5 %star.1 = (f32[2,128,128]{2,1,0:T(8,128)S(1)}, f32[464,128]{1,0:T(8,128)S(1)}, f32[464,128]{1,0:T(8,128)S(1)}, f32[2,12,224,256]{3,2,1,0:T(8,128)S(1)}) custom-call(s32[1]{0:T(128)S(6)} %copy.18.live, f32[32,16]{1,0:T(8,128)S(1)} %copy-done.4, f32[16,256]{1,0:T(8,128)S(1)} %column.1.order.refs_0_, ...), custom_call_target="tpu_custom_call", output_to_operand_aliasing={{1}: (11, {}), {2}: (12, {})} | custom-call | tf_op jit(solution)/shard_map/star/pallas_call | solution.py:476
  13.0 4.8 %collective-permute-start.3 = (f32[464,128]{1,0:T(8,128)S(1)}, f32[464,128]{1,0:T(8,128)S(1)}, u32[]{:S(2)}, u32[]{:S(2)}) collective-permute-start(f32[464,128]{1,0:T(8,128)S(1)} %get-tuple-element.26), channel_id=1, source_target_pairs={{0,252},{4,8},{8,4},{12,16},{16,12},{20,24},{24,20},{28,32},{32,28... | collective-permute-start | bytes 712712 | tf_op jit(solution)/shard_map/ppermute | solution.py:492
  17.8 0.0 collective-permute-start.4
  17.8 3.3 %inner.1 = (f32[2,128,128]{2,1,0:T(8,128)S(1)}, f32[2,12,224,256]{3,2,1,0:T(8,128)S(1)}, bf16[12,256,256]{2,1,0:T(8,128)(2,1)S(1)}) custom-call(s32[4,256]{1,0:T(4,128)S(1)} %copy-done.1, s32[4,256]{1,0:T(4,128)S(1)} %copy-done.2, f32[2,128,128]{2,1,0:T(8,128)S(1)} %get-tuple-element.20.star.order, ...), custom_call_target="tpu_custom_call", output_to_operand_aliasing={{1}: (4, {})} | custom-call | tf_op jit(solution)/shard_map/inner/pallas_call | solution.py:497
  21.0 0.9 %collective-permute-done.3.outside = f32[464,128]{1,0:T(8,128)S(1)} collective-permute-done((f32[464,128]{1,0:T(8,128)S(1)}, f32[464,128]{1,0:T(8,128)S(1)}, u32[]{:S(2)}, u32[]{:S(2)}) %collective-permute-start.3) | collective-permute-done | bytes 237600 | tf_op jit(solution)/shard_map/ppermute | solution.py:492
  22.0 0.0 collective-permute-done.4.inside
  22.0 4.6 %outer.1 = (f32[2,2,16,256]{3,2,1,0:T(8,128)}, f32[16,256]{1,0:T(8,128)}, f32[2,9,224,256]{3,2,1,0:T(8,128)}) custom-call(s32[1]{0:T(128)S(6)} %copy.18.live, s32[4,256]{1,0:T(4,128)S(1)} %copy-done.1, s32[4,256]{1,0:T(4,128)S(1)} %copy-done.2, f32[2,128,128]{2,1,0:T(8,128)S(1)} %get-tuple-element.22.sums, f32[2,9,224,256]{3,2,1,0:T(8,128)S(1)} %get-tuple-element.23.held, ...), custom_call_target="tpu_custom_call" | custom-call | tf_op jit(solution)/shard_map/outer/pallas_call | solution.py:511
Async XLA Ops:
  0.6 9.8 %copy-start.4 = (f32[32,16]{1,0:T(8,128)S(1)}, f32[32,16]{1,0:T(8,128)}, u32[]{:S(2)}) copy-start(f32[32,16]{1,0:T(8,128)} %constant.5.clone.matrix) | copy-start | bytes 6148
  0.6 9.8 %copy-start = (f32[2,2,16,256]{3,2,1,0:T(8,128)S(1)}, f32[2,2,16,256]{3,2,1,0:T(8,128)}, u32[]{:S(2)}) copy-start(f32[2,2,16,256]{3,2,1,0:T(8,128)} %refs_5_.1) | copy-start | bytes 196612
  0.7 9.8 %copy-start.2 = (s32[4,256]{1,0:T(4,128)S(1)}, s32[4,256]{1,0:T(4,128)}, u32[]{:S(2)}) copy-start(s32[4,256]{1,0:T(4,128)} %rotations.3) | copy-start | bytes 12292
  0.7 9.8 %copy-start.1 = (s32[4,256]{1,0:T(4,128)S(1)}, s32[4,256]{1,0:T(4,128)}, u32[]{:S(2)}) copy-start(s32[4,256]{1,0:T(4,128)} %neighbours.3) | copy-start | bytes 12292
  0.7 9.8 %copy-start.3 = (f32[16,256]{1,0:T(8,128)S(1)}, f32[16,256]{1,0:T(8,128)}, u32[]{:S(2)}) copy-start(f32[16,256]{1,0:T(8,128)} %refs_4_.1) | copy-start | bytes 49156
  1.8 8.7 %collective-permute-start.2 = (f32[16,256]{1,0:T(8,128)S(1)}, f32[16,256]{1,0:T(8,128)S(1)}, u32[]{:S(2)}, u32[]{:S(2)}) collective-permute-start(f32[16,256]{1,0:T(8,128)S(1)} %column.1.order.refs_0_), channel_id=1, source_target_pairs={{0,3},{1,2},{2,1},{3,0},{4,7},{5,6},{6,5},{7,4},{8,11},{9,10},{10,... | collective-permute-start | bytes 49160 | tf_op jit(solution)/shard_map/ppermute | solution.py:458
  2.4 8.0 %collective-permute-start.1 = (f32[16,256]{1,0:T(8,128)S(1)}, f32[16,256]{1,0:T(8,128)S(1)}, u32[]{:S(2)}, u32[]{:S(2)}) collective-permute-start(f32[16,256]{1,0:T(8,128)S(1)} %column.1.order.refs_0_), channel_id=1, source_target_pairs={{0,2},{1,3},{2,0},{3,1},{4,6},{5,7},{6,4},{7,5},{8,10},{9,11},{10,... | collective-permute-start | bytes 49160 | tf_op jit(solution)/shard_map/ppermute | solution.py:458
  5.1 5.3 %collective-permute-start = (f32[16,256]{1,0:T(8,128)S(1)}, f32[16,256]{1,0:T(8,128)S(1)}, u32[]{:S(2)}, u32[]{:S(2)}) collective-permute-start(f32[16,256]{1,0:T(8,128)S(1)} %column.1.order.refs_0_), channel_id=1, source_target_pairs={{0,1},{1,0},{2,3},{3,2},{4,5},{5,4},{6,7},{7,6},{8,9},{9,8},{10,11... | collective-permute-start | bytes 49160 | tf_op jit(solution)/shard_map/ppermute | solution.py:458
  13.0 8.9 %collective-permute-start.3 = (f32[464,128]{1,0:T(8,128)S(1)}, f32[464,128]{1,0:T(8,128)S(1)}, u32[]{:S(2)}, u32[]{:S(2)}) collective-permute-start(f32[464,128]{1,0:T(8,128)S(1)} %get-tuple-element.26), channel_id=1, source_target_pairs={{0,252},{4,8},{8,4},{12,16},{16,12},{20,24},{24,20},{28,32},{32,28... | collective-permute-start | bytes 712712 | tf_op jit(solution)/shard_map/ppermute | solution.py:492
  17.8 4.2 %collective-permute-start.4 = (f32[464,128]{1,0:T(8,128)S(1)}, f32[464,128]{1,0:T(8,128)S(1)}, u32[]{:S(2)}, u32[]{:S(2)}) collective-permute-start(f32[464,128]{1,0:T(8,128)S(1)} %get-tuple-element.27), channel_id=1, source_target_pairs={{0,4},{4,0},{8,12},{12,8},{16,20},{20,16},{24,28},{28,24},{32,36},... | collective-permute-start | bytes 712712 | tf_op jit(solution)/shard_map/ppermute | solution.py:495
